TPU v7x, 128 devices: a whole 4x4x4 slice. The times are simulated.
128 devices in a mesh: lat: 8 (over y, core), lon: 16 (over z, x).
Axes of the slice: x: 4, y: 4, z: 4, core: 2. Of those that a mesh axis runs over, the one named last changes fastest.
Arguments:
- background: bfloat16 [512, 1024, 128], P('lat', 'lon'), may hold values from -6 to 6
- diffusivity: float32 [512, 1024, 128], P('lat', 'lon'), may hold values from 0.12 to 0.245
- tile_index: int32 [65536, 1], P(('lat', 'lon')), may hold values from 0 to 127; in each aligned block of 512 rows (0 to 511, 512 to 1023, ...) at most 8 rows name the same one
- anchor: int32 [65536], P(('lat', 'lon')), may hold values from 0 to 3968
- weights: float32 [65536, 4], P(('lat', 'lon')), may hold values from 0.2 to 1
- observed: float32 [65536, 128], P(('lat', 'lon')), may hold values from -6 to 6
- accept: int32 [65536, 128], P(('lat', 'lon')), may hold values 0 or 1
- absorb: float32 [128, 128], replicated, may hold values from 0.001 to 0.1
- sensitivity: float32 [128], replicated, may hold values from -0.5 to 0.5
- inverse_variance: float32 [128], replicated, may hold values from 0.25 to 4
Outputs:
- departure: float32 [65536, 128], P(('lat', 'lon'))
- increment: float32 [512, 1024, 128], P('lat', 'lon')
Inputs may be any that keep to these rules, and one draw needn't show every extreme that they name: `tile_index`: among the 512 footprints of one device no tile is named more than 8 times, a bound that some block reaches.
All inputs are finite; a program needn't handle non-finite values. No bound on the sum of `accept` on one device may be relied on, other than what follows from the above.
Results may differ from a plain program's by a relative error of at most 0.0003.
Values may be sent and summed in bfloat16 or wider, within the bound.
A program may use at most 64 MiB of HBM per device.

v0:
```python
import jax
import jax.numpy as jnp
from jax import lax
from jax.sharding import PartitionSpec as P

STEPS = 8


NEIGHBOURS = ((-1, 0), (1, 0), (0, -1), (0, 1))


def padded_2(block, sides, width, periodic):
    for axis, dim in sides:
        count = lax.axis_size(axis)
        forward = [(i, i + 1) for i in range(count - 1)]
        if periodic:
            forward.append((count - 1, 0))
        backward = [(target, source) for source, target in forward]
        low = lax.ppermute(
            lax.slice_in_dim(block, block.shape[dim] - width, None, axis=dim), axis, forward
        )
        high = lax.ppermute(lax.slice_in_dim(block, 0, width, axis=dim), axis, backward)
        block = jnp.concatenate([low, block, high], axis=dim)
    return block


def evolve(profile, absorb, sensitivity):
    layer_depth = absorb[None, :, :] * jnp.exp(sensitivity[None, None, :] * profile[:, :, None])
    optical = jnp.cumsum(layer_depth, axis=1)
    transmit = jnp.exp(-optical)
    transmit_above = jnp.concatenate(
        [jnp.ones_like(transmit[:, :1, :]), transmit[:, :-1, :]], axis=1
    )
    layered = jnp.sum(profile[:, :, None] * (transmit_above - transmit), axis=1)
    return layered + profile[:, -1:] * transmit[:, -1, :]


def assess(profile, observed, accept, absorb, sensitivity, inverse_variance):
    evolved, pullback = jax.vjp(lambda prof_in: evolve(prof_in, absorb, sensitivity), profile)
    departure = observed - evolved
    (adjoint,) = pullback(-(accept.astype(jnp.float32) * inverse_variance[None, :] * departure))
    return (departure, adjoint)


def extend(grid_field, halo_width):
    padded = padded_2(grid_field, (("lat", 0),), halo_width, False)
    return padded_2(padded, (("lon", 1),), halo_width, True)


def relax(grid_field, diffusivity):
    height = grid_field.shape[0]
    breadth = grid_field.shape[1]
    centre = grid_field[1:-1, 1:-1]
    kappa_centre = diffusivity[1:-1, 1:-1]
    summed = centre
    for d_row, d_col in NEIGHBOURS:
        neighbour = grid_field[1 + d_row : height - 1 + d_row, 1 + d_col : breadth - 1 + d_col]
        kappa_near = diffusivity[1 + d_row : height - 1 + d_row, 1 + d_col : breadth - 1 + d_col]
        summed = summed + 0.5 * (kappa_centre + kappa_near) * (neighbour - centre)
    return summed


def local(
    background,
    diffusivity,
    tile_index,
    anchor,
    weights,
    observed,
    accept,
    absorb,
    sensitivity,
    inverse_variance,
):
    lat_count = lax.axis_size("lat")
    lon_count = lax.axis_size("lon")
    dev_count = lat_count * lon_count
    foot_count = tile_index.shape[0]
    capacity = max(2, 2 * foot_count // dev_count)
    tile_rows, tile_cols, levels = background.shape
    owner_tile = tile_index[:, 0]
    onehot = (owner_tile[:, None] == jnp.arange(dev_count, dtype=jnp.int32)[None, :]).astype(
        jnp.int32
    )
    slot_rank = jnp.sum((jnp.cumsum(onehot, axis=0) - onehot) * onehot, axis=1)
    slot_index = owner_tile * capacity + slot_rank
    base_cell = anchor // (tile_cols - 1) * tile_cols + anchor % (tile_cols - 1)
    local_ids = jnp.stack(
        [base_cell, base_cell + 1, base_cell + tile_cols, base_cell + tile_cols + 1], axis=1
    )
    shares = weights / jnp.sum(weights, axis=1, keepdims=True)
    request = (
        jnp.zeros((dev_count * capacity, 4), jnp.int32)
        .at[slot_index]
        .set(local_ids)
        .reshape(dev_count, capacity, 4)
    )
    asked_ids = lax.all_to_all(
        request, ("lat", "lon"), split_axis=0, concat_axis=0, tiled=True
    ).reshape(-1)
    flat_bg = background.reshape(tile_rows * tile_cols, levels)
    columns = jnp.take(flat_bg, asked_ids, axis=0).reshape(dev_count, capacity, 4, levels)
    share_slots = (
        jnp.zeros((dev_count * capacity, 4), jnp.float32)
        .at[slot_index]
        .set(shares)
        .reshape(dev_count, capacity, 4)
    )
    asked_shares = lax.all_to_all(
        share_slots, ("lat", "lon"), split_axis=0, concat_axis=0, tiled=True
    )
    local_profiles = jnp.sum(asked_shares[:, :, :, None] * columns.astype(jnp.float32), axis=2)
    returned = lax.all_to_all(
        local_profiles, ("lat", "lon"), split_axis=0, concat_axis=0, tiled=True
    )
    profile = returned.reshape(dev_count * capacity, levels)[slot_index]
    block_count = foot_count // 64
    channels = observed.shape[1]
    departure, adjoint = lax.map(
        lambda packed: assess(
            packed[0], packed[1], packed[2], absorb, sensitivity, inverse_variance
        ),
        (
            profile.reshape(block_count, 64, levels),
            observed.reshape(block_count, 64, channels),
            accept.reshape(block_count, 64, channels),
        ),
    )
    departure = departure.reshape(foot_count, channels)
    adjoint = adjoint.reshape(foot_count, levels)
    grad_slots = (
        jnp.zeros((dev_count * capacity, levels), jnp.float32)
        .at[slot_index]
        .set(adjoint)
        .reshape(dev_count, capacity, levels)
    )
    arrived = lax.all_to_all(grad_slots, ("lat", "lon"), split_axis=0, concat_axis=0, tiled=True)
    adjoint_terms = asked_shares[:, :, :, None] * arrived[:, :, None, :]
    increment = (
        jnp.zeros((tile_rows * tile_cols, levels), jnp.float32)
        .at[asked_ids]
        .add(-adjoint_terms.reshape(-1, levels))
    )
    grid_field = increment.reshape(tile_rows, tile_cols, levels)
    kappa_ext = extend(diffusivity, 2)
    first_row = lax.axis_index("lat") * tile_rows - 1
    row_global = first_row + jnp.arange(tile_rows + 2, dtype=jnp.int32)
    inside = ((row_global >= 0) & (row_global < lat_count * tile_rows)).astype(jnp.float32)[
        :, None, None
    ]
    for repeat_index in range(STEPS // 2):
        middle = relax(extend(grid_field, 2), kappa_ext) * inside
        grid_field = relax(middle, kappa_ext[1:-1, 1:-1])
    return (departure, grid_field)


def solution(mesh):
    in_specs = (
        P("lat", "lon", None),
        P("lat", "lon", None),
        P(("lat", "lon"), None),
        P(("lat", "lon")),
        P(("lat", "lon"), None),
        P(("lat", "lon"), None),
        P(("lat", "lon"), None),
        P(),
        P(),
        P(),
    )
    out_specs = (P(("lat", "lon"), None), P("lat", "lon", None))
    return jax.shard_map(local, mesh=mesh, in_specs=in_specs, out_specs=out_specs, check_vma=False)
```

profile of v0, /device:TPU:1, one launch (start us, length us, event | category | flops | bytes accessed | tf_op | source)
XLA Modules:
  0.0 472.8 jit_solution(8410901266364921809)
XLA Ops:
  7.7 11.5 %all-to-all-start.1 = ((s32[128,8,4]{1,2,0:T(4,128)}), s32[128,8,4]{1,2,0:T(4,128)S(1)}, u32[]{:S(2)}, u32[]{:S(2)}) async-start(s32[128,8,4]{1,2,0:T(4,128)} %copy.34), calls=%async_computation.1 | async-start | bytes 524288 | tf_op jit(solution)/shard_map/all_to_all | solution.py:98
  22.8 7.9 %all-to-all-done.1 = s32[128,8,4]{1,2,0:T(4,128)S(1)} async-done(((s32[128,8,4]{1,2,0:T(4,128)}), s32[128,8,4]{1,2,0:T(4,128)S(1)}, u32[]{:S(2)}, u32[]{:S(2)}) %all-to-all-start.1) | async-done | bytes 16416 | tf_op jit(solution)/shard_map/all_to_all | solution.py:98
  30.7 4.0 all-to-all-start
  36.9 12.1 %gather_fusion = bf16[4096,128]{1,0:T(8,128)(2,1)S(1)} fusion(bf16[4096,128]{1,0:T(8,128)(2,1)S(1)} %bitcast.112, s32[4096]{0:T(1024)S(1)} %broadcast_clamp_fusion), kind=kCustom, calls=%fused_computation | custom fusion | bytes 2113536 | tf_op jit(solution)/shard_map/jit(_take)/gather | solution.py:102
  49.9 3.6 multiply_reduce_fusion.3
  53.5 9.8 %all-to-all-start.2 = ((f32[128,8,128]{2,1,0:T(8,128)}), f32[128,8,128]{2,1,0:T(8,128)S(1)}, u32[]{:S(2)}, u32[]{:S(2)}) async-start(f32[128,8,128]{2,1,0:T(8,128)} %multiply_reduce_fusion.3), calls=%async_computation.2 | async-start | bytes 1048576 | tf_op jit(solution)/shard_map/all_to_all | solution.py:113
  63.4 14.1 %all-to-all-done.2 = f32[128,8,128]{2,1,0:T(8,128)S(1)} async-done(((f32[128,8,128]{2,1,0:T(8,128)}), f32[128,8,128]{2,1,0:T(8,128)S(1)}, u32[]{:S(2)}, u32[]{:S(2)}) %all-to-all-start.2) | async-done | bytes 524320 | tf_op jit(solution)/shard_map/all_to_all | solution.py:113
  78.5 233.5 %while.12 = (s32[]{:T(128)}, f32[8,64,128]{2,1,0:T(8,128)}, f32[8,64,128]{2,1,0:T(8,128)S(1)}, f32[8,64,128]{2,1,0:T(8,128)}, f32[8,64,128]{2,1,0:T(8,128)S(1)},...) while((s32[]{:T(128)}, f32[8,64,128]{2,1,0:T(8,128)}, ...), condition=%wide.region_14.15_spmd, body=%wide.region_7.14_spmd.sunk | while | flops 288513984 | bytes 68161688 | solution.py:119
  83.8 2.6 multiply_reduce_fusion.8
  86.7 19.6 %multiply_reduce_fusion.9 = f32[64,128]{0,1:T(8,128)S(1)} fusion(f32[128]{0:T(128)S(1)} %get-tuple-element.234, f32[128,128]{1,0:T(8,128)S(1)} %get-tuple-element.233, f32[64,128]{0,1:T(8,128)S(1)} %bitcast.117, f32[64,128,128]{2,0,1:T(8,128)S(1)} %negate_exponential_fusion.2, f32[64,127,128]{2,0,1:T(8,128)S(1)} %split.5, ...), kind=kOutput, calls=%fused_computation.6.clone.1 | output fusion | flops 144695296 | bytes 8552960 | tf_op jit(solution)/shard_map/while/body/eval_jaxpr/transpose(jvp(jit(cumsum)))/reduce_window_sum | solution.py:29
  112.9 2.6 multiply_reduce_fusion.8
  115.8 19.6 %multiply_reduce_fusion.9 = f32[64,128]{0,1:T(8,128)S(1)} fusion(f32[128]{0:T(128)S(1)} %get-tuple-element.234, f32[128,128]{1,0:T(8,128)S(1)} %get-tuple-element.233, f32[64,128]{0,1:T(8,128)S(1)} %bitcast.117, f32[64,128,128]{2,0,1:T(8,128)S(1)} %negate_exponential_fusion.2, f32[64,127,128]{2,0,1:T(8,128)S(1)} %split.5, ...), kind=kOutput, calls=%fused_computation.6.clone.1 | output fusion | flops 144695296 | bytes 8552960 | tf_op jit(solution)/shard_map/while/body/eval_jaxpr/transpose(jvp(jit(cumsum)))/reduce_window_sum | solution.py:29
  142.0 2.6 multiply_reduce_fusion.8
  144.9 19.6 %multiply_reduce_fusion.9 = f32[64,128]{0,1:T(8,128)S(1)} fusion(f32[128]{0:T(128)S(1)} %get-tuple-element.234, f32[128,128]{1,0:T(8,128)S(1)} %get-tuple-element.233, f32[64,128]{0,1:T(8,128)S(1)} %bitcast.117, f32[64,128,128]{2,0,1:T(8,128)S(1)} %negate_exponential_fusion.2, f32[64,127,128]{2,0,1:T(8,128)S(1)} %split.5, ...), kind=kOutput, calls=%fused_computation.6.clone.1 | output fusion | flops 144695296 | bytes 8552960 | tf_op jit(solution)/shard_map/while/body/eval_jaxpr/transpose(jvp(jit(cumsum)))/reduce_window_sum | solution.py:29
  171.1 2.6 multiply_reduce_fusion.8
  174.0 19.6 %multiply_reduce_fusion.9 = f32[64,128]{0,1:T(8,128)S(1)} fusion(f32[128]{0:T(128)S(1)} %get-tuple-element.234, f32[128,128]{1,0:T(8,128)S(1)} %get-tuple-element.233, f32[64,128]{0,1:T(8,128)S(1)} %bitcast.117, f32[64,128,128]{2,0,1:T(8,128)S(1)} %negate_exponential_fusion.2, f32[64,127,128]{2,0,1:T(8,128)S(1)} %split.5, ...), kind=kOutput, calls=%fused_computation.6.clone.1 | output fusion | flops 144695296 | bytes 8552960 | tf_op jit(solution)/shard_map/while/body/eval_jaxpr/transpose(jvp(jit(cumsum)))/reduce_window_sum | solution.py:29
  200.2 2.6 multiply_reduce_fusion.8
  203.2 19.6 %multiply_reduce_fusion.9 = f32[64,128]{0,1:T(8,128)S(1)} fusion(f32[128]{0:T(128)S(1)} %get-tuple-element.234, f32[128,128]{1,0:T(8,128)S(1)} %get-tuple-element.233, f32[64,128]{0,1:T(8,128)S(1)} %bitcast.117, f32[64,128,128]{2,0,1:T(8,128)S(1)} %negate_exponential_fusion.2, f32[64,127,128]{2,0,1:T(8,128)S(1)} %split.5, ...), kind=kOutput, calls=%fused_computation.6.clone.1 | output fusion | flops 144695296 | bytes 8552960 | tf_op jit(solution)/shard_map/while/body/eval_jaxpr/transpose(jvp(jit(cumsum)))/reduce_window_sum | solution.py:29
  229.3 2.6 multiply_reduce_fusion.8
  232.3 19.6 %multiply_reduce_fusion.9 = f32[64,128]{0,1:T(8,128)S(1)} fusion(f32[128]{0:T(128)S(1)} %get-tuple-element.234, f32[128,128]{1,0:T(8,128)S(1)} %get-tuple-element.233, f32[64,128]{0,1:T(8,128)S(1)} %bitcast.117, f32[64,128,128]{2,0,1:T(8,128)S(1)} %negate_exponential_fusion.2, f32[64,127,128]{2,0,1:T(8,128)S(1)} %split.5, ...), kind=kOutput, calls=%fused_computation.6.clone.1 | output fusion | flops 144695296 | bytes 8552960 | tf_op jit(solution)/shard_map/while/body/eval_jaxpr/transpose(jvp(jit(cumsum)))/reduce_window_sum | solution.py:29
  258.5 2.6 multiply_reduce_fusion.8
  261.4 19.6 %multiply_reduce_fusion.9 = f32[64,128]{0,1:T(8,128)S(1)} fusion(f32[128]{0:T(128)S(1)} %get-tuple-element.234, f32[128,128]{1,0:T(8,128)S(1)} %get-tuple-element.233, f32[64,128]{0,1:T(8,128)S(1)} %bitcast.117, f32[64,128,128]{2,0,1:T(8,128)S(1)} %negate_exponential_fusion.2, f32[64,127,128]{2,0,1:T(8,128)S(1)} %split.5, ...), kind=kOutput, calls=%fused_computation.6.clone.1 | output fusion | flops 144695296 | bytes 8552960 | tf_op jit(solution)/shard_map/while/body/eval_jaxpr/transpose(jvp(jit(cumsum)))/reduce_window_sum | solution.py:29
  287.6 2.6 multiply_reduce_fusion.8
  290.5 19.6 %multiply_reduce_fusion.9 = f32[64,128]{0,1:T(8,128)S(1)} fusion(f32[128]{0:T(128)S(1)} %get-tuple-element.234, f32[128,128]{1,0:T(8,128)S(1)} %get-tuple-element.233, f32[64,128]{0,1:T(8,128)S(1)} %bitcast.117, f32[64,128,128]{2,0,1:T(8,128)S(1)} %negate_exponential_fusion.2, f32[64,127,128]{2,0,1:T(8,128)S(1)} %split.5, ...), kind=kOutput, calls=%fused_computation.6.clone.1 | output fusion | flops 144695296 | bytes 8552960 | tf_op jit(solution)/shard_map/while/body/eval_jaxpr/transpose(jvp(jit(cumsum)))/reduce_window_sum | solution.py:29
  314.6 4.0 all-to-all-start.3
  319.4 3.1 collective-permute-start.5
  328.4 4.4 all-to-all-done.3
  334.7 26.3 %scatter_custom_fusion.3 = f32[4096,128]{1,0:T(8,128)} fusion(s32[4096]{0:T(1024)S(1)} %bitcast.132, f32[4096,128]{1,0:T(8,128)} %bitcast.122, f32[4096]{0:T(1024)S(1)} %mul.335, f32[]{:T(128)} %constant.50.clone.1), kind=kCustom, calls=%fused_computation.204 | custom fusion | flops 1572864 | bytes 4210692 | tf_op jit(solution)/shard_map/scatter-add | solution.py:142
  364.4 3.1 collective-permute-start
  368.2 4.2 collective-permute-start.7
  373.6 4.8 %collective-permute-start.3 = (f32[68,2,128]{2,1,0:T(2,128)S(1)}, f32[68,2,128]{2,1,0:T(2,128)S(1)}, u32[]{:S(2)}, u32[]{:S(2)}) collective-permute-start(f32[68,2,128]{2,1,0:T(2,128)S(1)} %get-tuple-element.128), channel_id=1, source_target_pairs={{1,0},{2,1},{3,2},{4,3},{5,4},{6,5},{7,6},{8,7},{9,8},{10,9},{11,1... | collective-permute-start | bytes 208904 | tf_op jit(solution)/shard_map/ppermute | solution.py:22
  382.7 10.2 %fusion.70 = (f32[66,66,128]{2,1,0:T(8,128)S(1)}, f32[66,66,128]{2,1,0:T(8,128)S(1)}, f32[66,66,128]{2,1,0:T(8,128)S(1)}, f32[66,66,128]{2,1,0:T(8,128)S(1)}, f32[66,66,128]{2,1,0:T(8,128)}) fusion(f32[68,2,128]{2,1,0:T(2,128)S(1)} %collective-permute-done.3, f32[2,64,128]{2,1,0:T(8,128)S(1)} %collective-permute-done.1, f32[64,64,128]{2,1,0:T(8,128)} %bitcast.119, ...), kind=kLoop, calls=%fused_computation.125 | loop fusion | flops 16169472 | bytes 29268232 | tf_op jit(solution)/shard_map/mul | solution.py:152
  392.9 4.5 fusion.105
  397.5 3.5 collective-permute-start.8
  402.9 3.6 collective-permute-done.9
  406.9 5.1 %collective-permute-start.11 = (f32[68,2,128]{2,1,0:T(2,128)S(1)}, f32[68,2,128]{2,1,0:T(2,128)S(1)}, u32[]{:S(2)}, u32[]{:S(2)}) collective-permute-start(f32[68,2,128]{2,1,0:T(2,128)S(1)} %get-tuple-element.124), channel_id=1, source_target_pairs={{1,0},{2,1},{3,2},{4,3},{5,4},{6,5},{7,6},{8,7},{9,8},{10,9},{11,1... | collective-permute-start | bytes 208904 | tf_op jit(solution)/shard_map/ppermute | solution.py:22
  414.0 3.8 fusion.59
  417.8 4.5 fusion.97
  422.4 3.2 collective-permute-start.12
  427.6 3.6 collective-permute-done.13
  431.4 5.3 %collective-permute-start.15 = (f32[68,2,128]{2,1,0:T(2,128)S(1)}, f32[68,2,128]{2,1,0:T(2,128)S(1)}, u32[]{:S(2)}, u32[]{:S(2)}) collective-permute-start(f32[68,2,128]{2,1,0:T(2,128)S(1)} %get-tuple-element.122), channel_id=1, source_target_pairs={{1,0},{2,1},{3,2},{4,3},{5,4},{6,5},{7,6},{8,7},{9,8},{10,9},{11,1... | collective-permute-start | bytes 208904 | tf_op jit(solution)/shard_map/ppermute | solution.py:22
  438.7 3.8 fusion.48
  442.5 4.5 fusion.89
  447.1 3.0 collective-permute-start.16
  452.0 3.6 collective-permute-done.17
  455.8 5.6 %collective-permute-start.19 = (f32[68,2,128]{2,1,0:T(2,128)S(1)}, f32[68,2,128]{2,1,0:T(2,128)S(1)}, u32[]{:S(2)}, u32[]{:S(2)}) collective-permute-start(f32[68,2,128]{2,1,0:T(2,128)S(1)} %get-tuple-element.120), channel_id=1, source_target_pairs={{1,0},{2,1},{3,2},{4,3},{5,4},{6,5},{7,6},{8,7},{9,8},{10,9},{11,1... | collective-permute-start | bytes 208904 | tf_op jit(solution)/shard_map/ppermute | solution.py:22
  463.2 3.8 fusion.37
  467.1 5.5 %fusion.81 = f32[64,64,128]{2,1,0:T(8,128)} fusion(f32[66,66,128]{2,1,0:T(8,128)S(1)} %fusion.37, f32[64,64,128]{2,1,0:T(8,128)S(1)} %copy-done.3, f32[2,64,128]{2,1,0:T(8,128)S(1)} %collective-permute-done.4, f32[2,64,128]{2,1,0:T(8,128)S(1)} %collective-permute-done.5, f32[68,64,128]{2,1,0:T(8,128)S(1)} %constant_dynamic-update-slice_fusion.1, ...), kind=kLoop, calls=%fused_computation.146 | loop fusion | flops 12582912 | bytes 17178624 | tf_op jit(solution)/shard_map/add | solution.py:59
  (214 shorter events, 102.1 us)
Async XLA Ops:
  0.6 36.3 %copy-start = (bf16[64,64,128]{2,1,0:T(8,128)(2,1)S(1)}, bf16[64,64,128]{2,1,0:T(8,128)(2,1)}, u32[]{:S(2)}) copy-start(bf16[64,64,128]{2,1,0:T(8,128)(2,1)} %param.12) | copy-start | bytes 3145732
  0.6 18.6 %copy-start.10 = (f32[512,4]{0,1:T(4,128)S(1)}, f32[512,4]{0,1:T(4,128)}, u32[]{:S(2)}) copy-start(f32[512,4]{0,1:T(4,128)} %param.16) | copy-start | bytes 24580
  7.7 23.0 %all-to-all-start.1 = ((s32[128,8,4]{1,2,0:T(4,128)}), s32[128,8,4]{1,2,0:T(4,128)S(1)}, u32[]{:S(2)}, u32[]{:S(2)}) async-start(s32[128,8,4]{1,2,0:T(4,128)} %copy.34), calls=%async_computation.1 | async-start | bytes 524288 | tf_op jit(solution)/shard_map/all_to_all | solution.py:98
  30.7 18.4 %all-to-all-start = ((f32[128,8,4]{1,2,0:T(4,128)}), f32[128,8,4]{1,2,0:T(4,128)S(1)}, u32[]{:S(2)}, u32[]{:S(2)}) async-start(f32[128,8,4]{1,2,0:T(4,128)} %copy.31), calls=%async_computation | async-start | bytes 524288 | tf_op jit(solution)/shard_map/all_to_all | solution.py:109
  49.9 3.7 copy-start.7
  49.9 28.6 %copy-start.6 = (f32[128,128]{1,0:T(8,128)S(1)}, f32[128,128]{1,0:T(8,128)}, u32[]{:S(2)}) copy-start(f32[128,128]{1,0:T(8,128)} %param.19) | copy-start | bytes 196612
  49.9 28.6 %copy-start.8 = (f32[128]{0:T(128)S(1)}, f32[128]{0:T(128)}, u32[]{:S(2)}) copy-start(f32[128]{0:T(128)} %param.20) | copy-start | bytes 1540
  49.9 28.6 %copy-start.9 = (f32[128]{0:T(128)S(1)}, f32[128]{0:T(128)}, u32[]{:S(2)}) copy-start(f32[128]{0:T(128)} %param.21) | copy-start | bytes 1540
  53.5 23.9 %all-to-all-start.2 = ((f32[128,8,128]{2,1,0:T(8,128)}), f32[128,8,128]{2,1,0:T(8,128)S(1)}, u32[]{:S(2)}, u32[]{:S(2)}) async-start(f32[128,8,128]{2,1,0:T(8,128)} %multiply_reduce_fusion.3), calls=%async_computation.2 | async-start | bytes 1048576 | tf_op jit(solution)/shard_map/all_to_all | solution.py:113
  80.0 6.7 %copy-start.2 = (f32[64,128,128]{2,0,1:T(8,128)}, f32[64,128,128]{2,0,1:T(8,128)S(1)}, u32[]{:S(2)}) copy-start(f32[64,128,128]{2,0,1:T(8,128)S(1)} %negate_exponential_fusion.2) | copy-start | bytes 12582916 | tf_op jit(solution)/shard_map/while
  109.1 6.7 %copy-start.2 = (f32[64,128,128]{2,0,1:T(8,128)}, f32[64,128,128]{2,0,1:T(8,128)S(1)}, u32[]{:S(2)}) copy-start(f32[64,128,128]{2,0,1:T(8,128)S(1)} %negate_exponential_fusion.2) | copy-start | bytes 12582916 | tf_op jit(solution)/shard_map/while
  138.3 6.7 %copy-start.2 = (f32[64,128,128]{2,0,1:T(8,128)}, f32[64,128,128]{2,0,1:T(8,128)S(1)}, u32[]{:S(2)}) copy-start(f32[64,128,128]{2,0,1:T(8,128)S(1)} %negate_exponential_fusion.2) | copy-start | bytes 12582916 | tf_op jit(solution)/shard_map/while
  167.4 6.7 %copy-start.2 = (f32[64,128,128]{2,0,1:T(8,128)}, f32[64,128,128]{2,0,1:T(8,128)S(1)}, u32[]{:S(2)}) copy-start(f32[64,128,128]{2,0,1:T(8,128)S(1)} %negate_exponential_fusion.2) | copy-start | bytes 12582916 | tf_op jit(solution)/shard_map/while
  196.5 6.7 %copy-start.2 = (f32[64,128,128]{2,0,1:T(8,128)}, f32[64,128,128]{2,0,1:T(8,128)S(1)}, u32[]{:S(2)}) copy-start(f32[64,128,128]{2,0,1:T(8,128)S(1)} %negate_exponential_fusion.2) | copy-start | bytes 12582916 | tf_op jit(solution)/shard_map/while
  225.6 6.7 %copy-start.2 = (f32[64,128,128]{2,0,1:T(8,128)}, f32[64,128,128]{2,0,1:T(8,128)S(1)}, u32[]{:S(2)}) copy-start(f32[64,128,128]{2,0,1:T(8,128)S(1)} %negate_exponential_fusion.2) | copy-start | bytes 12582916 | tf_op jit(solution)/shard_map/while
  254.7 6.7 %copy-start.2 = (f32[64,128,128]{2,0,1:T(8,128)}, f32[64,128,128]{2,0,1:T(8,128)S(1)}, u32[]{:S(2)}) copy-start(f32[64,128,128]{2,0,1:T(8,128)S(1)} %negate_exponential_fusion.2) | copy-start | bytes 12582916 | tf_op jit(solution)/shard_map/while
  283.8 6.7 %copy-start.2 = (f32[64,128,128]{2,0,1:T(8,128)}, f32[64,128,128]{2,0,1:T(8,128)S(1)}, u32[]{:S(2)}) copy-start(f32[64,128,128]{2,0,1:T(8,128)S(1)} %negate_exponential_fusion.2) | copy-start | bytes 12582916 | tf_op jit(solution)/shard_map/while
  314.6 18.2 %all-to-all-start.3 = ((f32[128,8,128]{2,1,0:T(8,128)}), f32[128,8,128]{2,1,0:T(8,128)S(1)}, u32[]{:S(2)}, u32[]{:S(2)}) async-start(f32[128,8,128]{2,1,0:T(8,128)} %bitcast.34), calls=%async_computation.3 | async-start | bytes 1048576 | tf_op jit(solution)/shard_map/all_to_all | solution.py:137
  319.4 8.9 %collective-permute-start.5 = (f32[2,64,128]{2,1,0:T(8,128)S(1)}, f32[2,64,128]{2,1,0:T(8,128)S(1)}, u32[]{:S(2)}, u32[]{:S(2)}) collective-permute-start(f32[2,64,128]{2,1,0:T(8,128)S(1)} %get-tuple-element.135), channel_id=1, source_target_pairs={{16,0},{32,16},{48,32},{64,48},{80,64},{96,80},{112,96},{17,1},{33... | collective-permute-start | bytes 196616 | tf_op jit(solution)/shard_map/ppermute | solution.py:22
  322.5 4.1 collective-permute-start.4
  361.9 10.5 %collective-permute-start.1 = (f32[2,64,128]{2,1,0:T(8,128)S(1)}, f32[2,64,128]{2,1,0:T(8,128)S(1)}, u32[]{:S(2)}, u32[]{:S(2)}) collective-permute-start(f32[2,64,128]{2,1,0:T(8,128)S(1)} %bitcast.134), channel_id=1, source_target_pairs={{16,0},{32,16},{48,32},{64,48},{80,64},{96,80},{112,96},{17,1},{33... | collective-permute-start | bytes 196616 | tf_op jit(solution)/shard_map/ppermute | solution.py:22
  364.4 8.0 %collective-permute-start = (f32[2,64,128]{2,1,0:T(8,128)S(1)}, f32[2,64,128]{2,1,0:T(8,128)S(1)}, u32[]{:S(2)}, u32[]{:S(2)}) collective-permute-start(f32[2,64,128]{2,1,0:T(8,128)S(1)} %bitcast.133), channel_id=1, source_target_pairs={{0,16},{16,32},{32,48},{48,64},{64,80},{80,96},{96,112},{1,17},{17... | collective-permute-start | bytes 196616 | tf_op jit(solution)/shard_map/ppermute | solution.py:19
  367.6 10.8 %collective-permute-start.6 = (f32[68,2,128]{2,1,0:T(2,128)S(1)}, f32[68,2,128]{2,1,0:T(2,128)S(1)}, u32[]{:S(2)}, u32[]{:S(2)}) collective-permute-start(f32[68,2,128]{2,1,0:T(2,128)S(1)} %get-tuple-element.125), channel_id=1, source_target_pairs={{0,1},{1,2},{2,3},{3,4},{4,5},{5,6},{6,7},{7,8},{8,9},{9,10},{10,1... | collective-permute-start | bytes 208904 | tf_op jit(solution)/shard_map/ppermute | solution.py:19
  368.2 10.2 %collective-permute-start.7 = (f32[68,2,128]{2,1,0:T(2,128)S(1)}, f32[68,2,128]{2,1,0:T(2,128)S(1)}, u32[]{:S(2)}, u32[]{:S(2)}) collective-permute-start(f32[68,2,128]{2,1,0:T(2,128)S(1)} %get-tuple-element.126), channel_id=1, source_target_pairs={{1,0},{2,1},{3,2},{4,3},{5,4},{6,5},{7,6},{8,7},{9,8},{10,9},{11,1... | collective-permute-start | bytes 208904 | tf_op jit(solution)/shard_map/ppermute | solution.py:22
  373.5 7.3 %collective-permute-start.2 = (f32[68,2,128]{2,1,0:T(2,128)S(1)}, f32[68,2,128]{2,1,0:T(2,128)S(1)}, u32[]{:S(2)}, u32[]{:S(2)}) collective-permute-start(f32[68,2,128]{2,1,0:T(2,128)S(1)} %get-tuple-element.127), channel_id=1, source_target_pairs={{0,1},{1,2},{2,3},{3,4},{4,5},{5,6},{6,7},{7,8},{8,9},{9,10},{10,1... | collective-permute-start | bytes 208904 | tf_op jit(solution)/shard_map/ppermute | solution.py:19
  373.6 7.2 %copy-start.5 = (f32[4096,128]{1,0:T(8,128)S(1)}, f32[4096,128]{1,0:T(8,128)}, u32[]{:S(2)}) copy-start(f32[4096,128]{1,0:T(8,128)} %scatter_custom_fusion.3) | copy-start | bytes 6291460
  373.6 7.2 %collective-permute-start.3 = (f32[68,2,128]{2,1,0:T(2,128)S(1)}, f32[68,2,128]{2,1,0:T(2,128)S(1)}, u32[]{:S(2)}, u32[]{:S(2)}) collective-permute-start(f32[68,2,128]{2,1,0:T(2,128)S(1)} %get-tuple-element.128), channel_id=1, source_target_pairs={{1,0},{2,1},{3,2},{4,3},{5,4},{6,5},{7,6},{8,7},{9,8},{10,9},{11,1... | collective-permute-start | bytes 208904 | tf_op jit(solution)/shard_map/ppermute | solution.py:22
  382.7 10.2 %copy-start.3 = (f32[64,64,128]{2,1,0:T(8,128)S(1)}, f32[64,64,128]{2,1,0:T(8,128)}, u32[]{:S(2)}) copy-start(f32[64,64,128]{2,1,0:T(8,128)} %param.13) | copy-start | bytes 6291460
  397.5 5.5 %collective-permute-start.8 = (f32[2,64,128]{2,1,0:T(8,128)S(1)}, f32[2,64,128]{2,1,0:T(8,128)S(1)}, u32[]{:S(2)}, u32[]{:S(2)}) collective-permute-start(f32[2,64,128]{2,1,0:T(8,128)S(1)} %get-tuple-element.133), channel_id=1, source_target_pairs={{0,16},{16,32},{32,48},{48,64},{64,80},{80,96},{96,112},{1,17},{17... | collective-permute-start | bytes 196616 | tf_op jit(solution)/shard_map/ppermute | solution.py:19
  401.0 5.6 %collective-permute-start.9 = (f32[2,64,128]{2,1,0:T(8,128)S(1)}, f32[2,64,128]{2,1,0:T(8,128)S(1)}, u32[]{:S(2)}, u32[]{:S(2)}) collective-permute-start(f32[2,64,128]{2,1,0:T(8,128)S(1)} %get-tuple-element.134), channel_id=1, source_target_pairs={{16,0},{32,16},{48,32},{64,48},{80,64},{96,80},{112,96},{17,1},{33... | collective-permute-start | bytes 196616 | tf_op jit(solution)/shard_map/ppermute | solution.py:22
  406.6 7.0 %collective-permute-start.10 = (f32[68,2,128]{2,1,0:T(2,128)S(1)}, f32[68,2,128]{2,1,0:T(2,128)S(1)}, u32[]{:S(2)}, u32[]{:S(2)}) collective-permute-start(f32[68,2,128]{2,1,0:T(2,128)S(1)} %get-tuple-element.123), channel_id=1, source_target_pairs={{0,1},{1,2},{2,3},{3,4},{4,5},{5,6},{6,7},{7,8},{8,9},{9,10},{10,1... | collective-permute-start | bytes 208904 | tf_op jit(solution)/shard_map/ppermute | solution.py:19
  406.9 7.1 %copy-start.4 = (f32[66,66,128]{2,1,0:T(8,128)S(1)}, f32[66,66,128]{2,1,0:T(8,128)}, u32[]{:S(2)}) copy-start(f32[66,66,128]{2,1,0:T(8,128)} %get-tuple-element.112) | copy-start | bytes 6690820
  406.9 6.7 %collective-permute-start.11 = (f32[68,2,128]{2,1,0:T(2,128)S(1)}, f32[68,2,128]{2,1,0:T(2,128)S(1)}, u32[]{:S(2)}, u32[]{:S(2)}) collective-permute-start(f32[68,2,128]{2,1,0:T(2,128)S(1)} %get-tuple-element.124), channel_id=1, source_target_pairs={{1,0},{2,1},{3,2},{4,3},{5,4},{6,5},{7,6},{8,7},{9,8},{10,9},{11,1... | collective-permute-start | bytes 208904 | tf_op jit(solution)/shard_map/ppermute | solution.py:22
  422.4 5.2 %collective-permute-start.12 = (f32[2,64,128]{2,1,0:T(8,128)S(1)}, f32[2,64,128]{2,1,0:T(8,128)S(1)}, u32[]{:S(2)}, u32[]{:S(2)}) collective-permute-start(f32[2,64,128]{2,1,0:T(8,128)S(1)} %get-tuple-element.131), channel_id=1, source_target_pairs={{0,16},{16,32},{32,48},{48,64},{64,80},{80,96},{96,112},{1,17},{17... | collective-permute-start | bytes 196616 | tf_op jit(solution)/shard_map/ppermute | solution.py:19
  425.6 5.6 %collective-permute-start.13 = (f32[2,64,128]{2,1,0:T(8,128)S(1)}, f32[2,64,128]{2,1,0:T(8,128)S(1)}, u32[]{:S(2)}, u32[]{:S(2)}) collective-permute-start(f32[2,64,128]{2,1,0:T(8,128)S(1)} %get-tuple-element.132), channel_id=1, source_target_pairs={{16,0},{32,16},{48,32},{64,48},{80,64},{96,80},{112,96},{17,1},{33... | collective-permute-start | bytes 196616 | tf_op jit(solution)/shard_map/ppermute | solution.py:22
  431.3 7.0 %collective-permute-start.14 = (f32[68,2,128]{2,1,0:T(2,128)S(1)}, f32[68,2,128]{2,1,0:T(2,128)S(1)}, u32[]{:S(2)}, u32[]{:S(2)}) collective-permute-start(f32[68,2,128]{2,1,0:T(2,128)S(1)} %get-tuple-element.121), channel_id=1, source_target_pairs={{0,1},{1,2},{2,3},{3,4},{4,5},{5,6},{6,7},{7,8},{8,9},{9,10},{10,1... | collective-permute-start | bytes 208904 | tf_op jit(solution)/shard_map/ppermute | solution.py:19
  431.4 6.9 %collective-permute-start.15 = (f32[68,2,128]{2,1,0:T(2,128)S(1)}, f32[68,2,128]{2,1,0:T(2,128)S(1)}, u32[]{:S(2)}, u32[]{:S(2)}) collective-permute-start(f32[68,2,128]{2,1,0:T(2,128)S(1)} %get-tuple-element.122), channel_id=1, source_target_pairs={{1,0},{2,1},{3,2},{4,3},{5,4},{6,5},{7,6},{8,7},{9,8},{10,9},{11,1... | collective-permute-start | bytes 208904 | tf_op jit(solution)/shard_map/ppermute | solution.py:22
  447.1 4.9 %collective-permute-start.16 = (f32[2,64,128]{2,1,0:T(8,128)S(1)}, f32[2,64,128]{2,1,0:T(8,128)S(1)}, u32[]{:S(2)}, u32[]{:S(2)}) collective-permute-start(f32[2,64,128]{2,1,0:T(8,128)S(1)} %get-tuple-element.129), channel_id=1, source_target_pairs={{0,16},{16,32},{32,48},{48,64},{64,80},{80,96},{96,112},{1,17},{17... | collective-permute-start | bytes 196616 | tf_op jit(solution)/shard_map/ppermute | solution.py:19
  450.1 5.6 %collective-permute-start.17 = (f32[2,64,128]{2,1,0:T(8,128)S(1)}, f32[2,64,128]{2,1,0:T(8,128)S(1)}, u32[]{:S(2)}, u32[]{:S(2)}) collective-permute-start(f32[2,64,128]{2,1,0:T(8,128)S(1)} %get-tuple-element.130), channel_id=1, source_target_pairs={{16,0},{32,16},{48,32},{64,48},{80,64},{96,80},{112,96},{17,1},{33... | collective-permute-start | bytes 196616 | tf_op jit(solution)/shard_map/ppermute | solution.py:22
  455.7 7.1 %collective-permute-start.18 = (f32[68,2,128]{2,1,0:T(2,128)S(1)}, f32[68,2,128]{2,1,0:T(2,128)S(1)}, u32[]{:S(2)}, u32[]{:S(2)}) collective-permute-start(f32[68,2,128]{2,1,0:T(2,128)S(1)} %get-tuple-element.119), channel_id=1, source_target_pairs={{0,1},{1,2},{2,3},{3,4},{4,5},{5,6},{6,7},{7,8},{8,9},{9,10},{10,1... | collective-permute-start | bytes 208904 | tf_op jit(solution)/shard_map/ppermute | solution.py:19
  455.8 7.0 %collective-permute-start.19 = (f32[68,2,128]{2,1,0:T(2,128)S(1)}, f32[68,2,128]{2,1,0:T(2,128)S(1)}, u32[]{:S(2)}, u32[]{:S(2)}) collective-permute-start(f32[68,2,128]{2,1,0:T(2,128)S(1)} %get-tuple-element.120), channel_id=1, source_target_pairs={{1,0},{2,1},{3,2},{4,3},{5,4},{6,5},{7,6},{8,7},{9,8},{10,9},{11,1... | collective-permute-start | bytes 208904 | tf_op jit(solution)/shard_map/ppermute | solution.py:22
  467.1 5.5 %copy-start.1 = (bf16[64,64,128]{2,1,0:T(8,128)(2,1)S(1)}, bf16[64,64,128]{2,1,0:T(8,128)(2,1)}, u32[]{:S(2)}) copy-start(bf16[64,64,128]{2,1,0:T(8,128)(2,1)} %param.12) | copy-start | bytes 3145732
where the time goes:
time: 481 us; the launch traced here: 473 us
  other arithmetic  306 us (64%)
  starting transfers between devices  82 us (17%)
  waiting for transfers between devices  42.8 us (9%)
  local copies, waits for them, and re-layouts  39.4 us (8%)
    another operation x16, other arithmetic, evolve(): optical = jnp.cumsum(layer_depth, axis=1)  166 us
    ppermute x10, starting transfers between devices, padded_2(): lax.ppermute(lax.slice_in_dim(block, 0, width, axis=dim), axis, backward)  36.3 us
    reduce_sum x16, other arithmetic, evolve(): layered = jnp.sum(profile[:, :, None] * (transmit_above - transmit), axis=1)  33.4 us
    scatter-add x1, other arithmetic, local(): increment = jnp.zeros((tile_rows * tile_cols, levels), jnp.float32).at[as...  26.3 us
    mul x4, other arithmetic, local(): middle = relax(extend(grid_field, 2), kappa_ext) * inside  21.6 us
    add x4, other arithmetic, relax(): summed = summed + 0.5 * (kappa_centre + kappa_near) * (neighbour - centre)  19.1 us
    ppermute x10, starting transfers between devices, padded_2(): lax.ppermute(lax.slice_in_dim(block, block.shape[dim] - width, None, axis...  16.4 us
    all_to_all x1, waiting for transfers between devices, local(): lax.all_to_all(local_profiles, ('lat', 'lon'), split_axis=0, concat_axis=...  14.1 us
  transfers between devices with their start and end apart: 24, of which 11 were waited for; matrix products, arithmetic and copies ran while one was open for 5% of the time, Pallas kernels for 0%

commit v1 on v0

v1 whole, which is shorter than its diff:
```python
import functools

import jax
import jax.numpy as jnp
from jax import lax
from jax.experimental import pallas as pl
from jax.experimental.pallas import tpu as pltpu
from jax.sharding import PartitionSpec as P

STEPS = 8
HALO = 8
SUB = 8
LANES = 128
LOG2E = 1.4426950408889634
LN2 = 0.6931471805599453
FIXED = 2.0**30
F32 = jnp.float32
BF16 = jnp.bfloat16
I32 = jnp.int32
MESH = pl.DeviceIdType.MESH
VMEM_SPEC = pl.BlockSpec(memory_space=pltpu.VMEM)
SMEM_SPEC = pl.BlockSpec(memory_space=pltpu.SMEM)
ANY_SPEC = pl.BlockSpec(memory_space=pl.ANY)
VMEM_BYTES = 56 * 2**20


def pieces(x):
    high = x.astype(BF16)
    rest = x - high.astype(F32)
    middle = rest.astype(BF16)
    low = (rest - middle.astype(F32)).astype(BF16)
    return high, middle, low


def dot(a, b, contract):
    return lax.dot_general(a, b, (contract, ((), ())), preferred_element_type=F32)


def request_kernel(cap, tile_ref, anchor_ref, weights_ref, slot_ref, request_ref):
    dev_count, _, width = request_ref.shape
    feet = tile_ref.shape[1]
    tile = tile_ref[...]
    named = lax.broadcasted_iota(I32, (dev_count, feet), 0) == tile
    onehot = named.astype(F32).astype(BF16)
    before = (
        lax.broadcasted_iota(I32, (feet, feet), 0) < lax.broadcasted_iota(I32, (feet, feet), 1)
    )
    earlier = dot(onehot, before.astype(F32).astype(BF16), ((1,), (0,)))
    rank = jnp.sum(jnp.where(named, earlier, 0.0), axis=0, keepdims=True).astype(I32)
    slot_ref[...] = tile * cap + rank
    anchor = anchor_ref[...]
    row = ((anchor.astype(F32) + 0.5) * (1.0 / 63.0)).astype(I32)
    base = (anchor + row).astype(F32)
    weights = weights_ref[...]
    shares = weights / jnp.sum(weights, axis=0, keepdims=True)
    place = lax.broadcasted_iota(I32, (cap, feet), 0) == rank
    fields = [base] + [shares[k : k + 1, :] for k in range(4)]
    rows = [jnp.where(place, field, 0.0) for field in fields]
    if width > 5 * cap:
        rows.append(jnp.zeros((width - 5 * cap, feet), F32))
    packed = jnp.concatenate(rows, axis=0)
    high, middle, low = pieces(packed)
    last = ((1,), (1,))
    message = dot(onehot, high, last) + dot(onehot, middle, last) + dot(onehot, low, last)
    scaled = jnp.where(
        lax.broadcasted_iota(I32, (dev_count, width), 1) < cap, message, message * FIXED
    )
    request_ref[...] = scaled.astype(I32).reshape(dev_count, 1, width)


def coordinates(index, lon_count):
    return (index // lon_count, lax.rem(index, lon_count))


def my_index(lon_count):
    return lax.axis_index("lat") * lon_count + lax.axis_index("lon")


def greet_all(me, dev_count, lon_count):
    barrier = pltpu.get_barrier_semaphore()

    @pl.loop(1, dev_count)
    def _(d):
        other = lax.rem(me + d, dev_count)
        pl.semaphore_signal(
            barrier, inc=1, device_id=coordinates(other, lon_count), device_id_type=MESH
        )

    return barrier


def columns_kernel(
    cap,
    lon_count,
    request_ref,
    background_ref,
    asked_ref,
    profile_ref,
    field,
    found,
    asked_smem,
    ask_send,
    ask_recv,
    back_send,
    back_recv,
    local_sem,
):
    dev_count = request_ref.shape[0]
    me = my_index(lon_count)
    tile_cols = 64
    barrier = greet_all(me, dev_count, lon_count)

    chunk = 256

    @pl.loop(0, background_ref.shape[0] // chunk)
    def _(j):
        at = pl.ds(pl.multiple_of(j * chunk, chunk), chunk)
        field[at, :] = background_ref[at, :].astype(F32)

    pl.semaphore_wait(barrier, dev_count - 1)

    def ask(other):
        return pltpu.make_async_remote_copy(
            src_ref=request_ref.at[other],
            dst_ref=asked_ref.at[me],
            send_sem=ask_send.at[other],
            recv_sem=ask_recv.at[me],
            device_id=coordinates(other, lon_count),
            device_id_type=MESH,
        )

    def ask_from(other):
        return pltpu.make_async_remote_copy(
            src_ref=request_ref.at[other],
            dst_ref=asked_ref.at[other],
            send_sem=ask_send.at[other],
            recv_sem=ask_recv.at[other],
            device_id=coordinates(other, lon_count),
            device_id_type=MESH,
        )

    @pl.loop(1, dev_count)
    def _(d):
        ask(lax.rem(me + d, dev_count)).start()

    asked_ref[me] = request_ref[me]

    @pl.loop(1, dev_count)
    def _(d):
        ask_from(lax.rem(me + d, dev_count)).wait_recv()

    to_smem = pltpu.make_async_copy(asked_ref, asked_smem, local_sem)
    to_smem.start()
    to_smem.wait()

    def gather(source):
        for r in range(cap):
            at = asked_smem[source, 0, r]
            total = None
            for k, offset in enumerate((0, 1, tile_cols, tile_cols + 1)):
                share = asked_smem[source, 0, (k + 1) * cap + r].astype(F32)
                term = share * field[pl.ds(at + offset, 1), :]
                total = term if total is None else total + term
            found[source, r : r + 1, :] = total * (1.0 / FIXED)

    def back(source):
        return pltpu.make_async_remote_copy(
            src_ref=found.at[source],
            dst_ref=profile_ref.at[me],
            send_sem=back_send.at[source],
            recv_sem=back_recv.at[me],
            device_id=coordinates(source, lon_count),
            device_id_type=MESH,
        )

    def back_from(other):
        return pltpu.make_async_remote_copy(
            src_ref=found.at[other],
            dst_ref=profile_ref.at[other],
            send_sem=back_send.at[other],
            recv_sem=back_recv.at[other],
            device_id=coordinates(other, lon_count),
            device_id_type=MESH,
        )

    @pl.loop(1, dev_count)
    def _(d):
        source = lax.rem(me + d, dev_count)
        gather(source)
        back(source).start()

    gather(me)
    profile_ref[me] = found[me]

    @pl.loop(1, dev_count)
    def _(d):
        other = lax.rem(me + d, dev_count)
        ask(other).wait_send()
        back(other).wait_send()
        back_from(other).wait_recv()


def exchange_kernel(lon_count, given_ref, taken_ref, send, recv):
    dev_count = given_ref.shape[0]
    me = my_index(lon_count)
    barrier = greet_all(me, dev_count, lon_count)
    taken_ref[me] = given_ref[me]
    pl.semaphore_wait(barrier, dev_count - 1)

    def give(other):
        return pltpu.make_async_remote_copy(
            src_ref=given_ref.at[other],
            dst_ref=taken_ref.at[me],
            send_sem=send.at[other],
            recv_sem=recv.at[me],
            device_id=coordinates(other, lon_count),
            device_id_type=MESH,
        )

    def take(other):
        return pltpu.make_async_remote_copy(
            src_ref=given_ref.at[other],
            dst_ref=taken_ref.at[other],
            send_sem=send.at[other],
            recv_sem=recv.at[other],
            device_id=coordinates(other, lon_count),
            device_id_type=MESH,
        )

    @pl.loop(1, dev_count)
    def _(d):
        give(lax.rem(me + d, dev_count)).start()

    @pl.loop(1, dev_count)
    def _(d):
        other = lax.rem(me + d, dev_count)
        give(other).wait_send()
        take(other).wait_recv()


def assess_kernel(
    slot_ref,
    arrived_ref,
    observed_ref,
    accept_ref,
    absorb_ref,
    sensitivity_ref,
    variance_ref,
    departure_ref,
    grad_ref,
    chosen,
    profile,
    slope,
    weight,
    absorb_wide,
    sens_log,
    sens_ln,
    depth,
    transmit,
    sums,
    adjoint,
):
    slots, levels = arrived_ref.shape
    feet, channels = observed_ref.shape
    groups = feet // LANES
    parts = channels // SUB

    wide = lambda row: jnp.swapaxes(jnp.broadcast_to(row, (LANES, channels)), 0, 1)
    sens = wide(sensitivity_ref[...])
    sens_log[...] = sens * LOG2E
    sens_ln[...] = sens * LN2

    absorb_t = jnp.swapaxes(absorb_ref[...] * (-LOG2E), 0, 1)

    @pl.loop(0, levels // SUB)
    def _(j):
        turned = pltpu.roll(absorb_t, lax.rem(levels - j * SUB, levels), 1)
        for i in range(SUB):
            absorb_wide[j * SUB + i] = jnp.broadcast_to(turned[:, i : i + 1], (channels, LANES))

    block = 256 if slots % 256 == 0 else slots

    @pl.loop(0, slots // block)
    def _(j):
        first = pl.multiple_of(j * block, block)
        here = lax.broadcasted_iota(I32, (block, feet), 0) + first == slot_ref[...]
        chosen[pl.ds(first, block), :] = here.astype(F32).astype(BF16)

    arrived_t = jnp.swapaxes(arrived_ref[...], 0, 1)
    high, middle, low = pieces(arrived_t)
    plain = ((1,), (0,))
    mine = dot(high, chosen[...], plain) + dot(middle, chosen[...], plain) + dot(low, chosen[...], plain)
    below = jnp.concatenate([mine[1:, :], mine[levels - 1 :, :]], axis=0)
    for g in range(groups):
        at = slice(g * LANES, (g + 1) * LANES)
        profile[g] = mine[:, at]
        slope[g] = below[:, at] - mine[:, at]

    for g in range(groups):
        at = pl.ds(g * LANES, LANES)
        accepted = accept_ref[at, :].astype(F32) * variance_ref[...]
        weight[:, at] = jnp.swapaxes(accepted, 0, 1)

    level = lax.broadcasted_iota(I32, (levels, levels * SUB), 0)
    source = lax.broadcasted_iota(I32, (levels, levels * SUB), 1) // SUB
    same = (level == source).astype(F32)
    fall = (level == source + 1).astype(F32) - jnp.where(level == levels - 1, 0.0, same)
    same = same.astype(BF16)
    fall = fall.astype(BF16)

    for g in range(groups):
        at = pl.ds(g * LANES, LANES)

        def descend(l, carry):
            p = profile[g, pl.ds(l, 1), :]
            q = slope[g, pl.ds(l, 1), :]
            out = []
            for c in range(parts):
                rows = slice(c * SUB, (c + 1) * SUB)
                optical, evolved = carry[c]
                layer = absorb_wide[l, rows, :] * jnp.exp2(sens_log[rows, :] * p)
                optical = optical + layer
                passed = jnp.exp2(optical)
                depth[l, rows, :] = layer
                transmit[l, rows, :] = passed
                out.append((optical, evolved + q * passed))
            return tuple(out)

        zero = jnp.zeros((SUB, LANES), F32)
        done = lax.fori_loop(0, levels, descend, ((zero, zero),) * parts, unroll=2)
        top = profile[g, 0:1, :]
        observed_t = jnp.swapaxes(observed_ref[at, :], 0, 1)
        departed = []
        pulls = []
        for c in range(parts):
            rows = slice(c * SUB, (c + 1) * SUB)
            part = observed_t[rows, :] - (done[c][1] + top)
            departed.append(part)
            pulls.append(-(weight[rows, at] * part))
        departure_ref[at, :] = jnp.swapaxes(jnp.concatenate(departed, axis=0), 0, 1)
        whole = pulls[0]
        for c in range(1, parts):
            whole = whole + pulls[c]
        whole = jnp.sum(whole, axis=0, keepdims=True)
        transmit_pull = tuple(pulls)

        def ascend(step, carry):
            l = levels - 1 - step
            q = slope[g, pl.ds(l, 1), :]
            out = []
            passed_sum = None
            layer_sum = None
            for c in range(parts):
                rows = slice(c * SUB, (c + 1) * SUB)
                pulled = transmit_pull[c] * transmit[l, rows, :]
                rest = carry[c] + q * pulled
                through = sens_ln[rows, :] * (depth[l, rows, :] * rest)
                passed_sum = pulled if c == 0 else passed_sum + pulled
                layer_sum = through if c == 0 else layer_sum + through
                out.append(rest)
            at_l = pl.ds(pl.multiple_of(l * SUB, SUB), SUB)
            sums[0, at_l, :] = passed_sum
            sums[1, at_l, :] = layer_sum
            return tuple(out)

        lax.fori_loop(0, levels, ascend, (zero,) * parts, unroll=2)
        total = None
        for matrix, index in ((fall, 0), (same, 1)):
            for piece in pieces(sums[index]):
                term = dot(matrix, piece, plain)
                total = term if total is None else total + term
        first = lax.broadcasted_iota(I32, (levels, LANES), 0) == 0
        adjoint[:, at] = total + jnp.where(first, whole, 0.0)

    parts_adjoint = pieces(adjoint[...])

    @pl.loop(0, slots // block)
    def _(j):
        rows = pl.ds(pl.multiple_of(j * block, block), block)
        total = None
        for piece in parts_adjoint:
            term = dot(chosen[rows, :], piece, ((1,), (1,)))
            total = term if total is None else total + term
        grad_ref[rows, :] = total


def spread_kernel(cap, asked_ref, arrived_ref, raw_ref, other):
    tile_cols = 64
    cells, levels = raw_ref.shape
    chunk = 256

    @pl.loop(0, cells // chunk)
    def _(j):
        at = pl.ds(pl.multiple_of(j * chunk, chunk), chunk)
        raw_ref[at, :] = jnp.zeros((chunk, levels), F32)
        other[at, :] = jnp.zeros((chunk, levels), F32)

    @pl.loop(0, asked_ref.shape[0])
    def _(source):
        for r in range(0, cap, 2):
            for total, row in ((raw_ref, r), (other, r + 1)):
                at = asked_ref[source, 0, row]
                value = arrived_ref[source, row : row + 1, :]
                sites = [pl.ds(at + o, 1) for o in (0, 1, tile_cols, tile_cols + 1)]
                fresh = []
                for k in range(4):
                    share = asked_ref[source, 0, (k + 1) * cap + row].astype(F32)
                    fresh.append(total[sites[k], :] + share * value)
                for k in range(4):
                    total[sites[k], :] = fresh[k]

    @pl.loop(0, cells // chunk)
    def _(j):
        at = pl.ds(pl.multiple_of(j * chunk, chunk), chunk)
        raw_ref[at, :] = (raw_ref[at, :] + other[at, :]) * (-1.0 / FIXED)


def diffuse_kernel(
    lat_count,
    lon_count,
    raw_ref,
    kappa_ref,
    out_ref,
    field_in,
    kappa_in,
    field,
    east,
    south,
    local_sems,
    send_sems,
    recv_sems,
):
    height, breadth, levels = raw_ref.shape
    tall = height + 2 * HALO
    count = (breadth + 2 * HALO) // SUB
    lat = lax.axis_index("lat")
    lon = lax.axis_index("lon")
    is_first = lat == 0
    is_last = lat == lat_count - 1

    directions = [(a, b) for a in (-1, 0, 1) for b in (-1, 0, 1) if (a, b) != (0, 0)]

    def there(a):
        return jnp.logical_and(lat + a >= 0, lat + a < lat_count)

    def device(a, b):
        return (lat + a, lax.rem(lon + b + lon_count, lon_count))

    barrier = pltpu.get_barrier_semaphore()
    for a, b in directions:

        @pl.when(there(a))
        def _(a=a, b=b):
            pl.semaphore_signal(barrier, inc=1, device_id=device(a, b), device_id_type=MESH)

    own = []
    centre = (pl.ds(HALO, height), pl.ds(HALO, breadth))
    for n, (source, target) in enumerate(((kappa_ref, kappa_in), (raw_ref, field_in))):
        copy = pltpu.make_async_copy(source, target.at[centre], local_sems.at[n])
        copy.start()
        own.append(copy)

    zero_rows = jnp.zeros((HALO, breadth + 2 * HALO, levels), F32)
    flat_rows = jnp.zeros((HALO, count, SUB, levels), F32)

    @pl.when(is_first)
    def _():
        kappa_in[pl.ds(0, HALO)] = zero_rows
        field_in[pl.ds(0, HALO)] = zero_rows
        field[pl.ds(0, HALO)] = flat_rows

    @pl.when(is_last)
    def _():
        kappa_in[pl.ds(HALO + height, HALO)] = zero_rows
        field_in[pl.ds(HALO + height, HALO)] = zero_rows
        field[pl.ds(HALO + height, HALO)] = flat_rows

    neighbours = 8 - 3 * is_first.astype(I32) - 3 * is_last.astype(I32)
    pl.semaphore_wait(barrier, neighbours)

    def span(step, size):
        given = {-1: pl.ds(0, HALO), 0: pl.ds(0, size), 1: pl.ds(size - HALO, HALO)}[step]
        taken = {-1: pl.ds(HALO + size, HALO), 0: pl.ds(HALO, size), 1: pl.ds(0, HALO)}[step]
        return given, taken

    def edge(array, n):
        a, b = directions[n]
        source, target = ((kappa_ref, kappa_in), (raw_ref, field_in))[array]
        given_rows, taken_rows = span(a, height)
        given_cols, taken_cols = span(b, breadth)
        return pltpu.make_async_remote_copy(
            src_ref=source.at[given_rows, given_cols],
            dst_ref=target.at[taken_rows, taken_cols],
            send_sem=send_sems.at[array, n],
            recv_sem=recv_sems.at[array, n],
            device_id=device(a, b),
            device_id_type=MESH,
        )

    for array in range(2):
        for n, (a, b) in enumerate(directions):

            @pl.when(there(a))
            def _(array=array, n=n):
                edge(array, n).start()

    def arrive(array):
        own[array].wait()
        for n, (a, b) in enumerate(directions):

            @pl.when(there(-a))
            def _(n=n):
                edge(array, n).wait_recv()

    def strided(ref, r):
        return tuple(ref[r, pl.ds(i, SUB, stride=count), :] for i in range(count))

    def later(x):
        return pltpu.roll(x, SUB - 1, 0)

    def sooner(x):
        return pltpu.roll(x, 1, 0)

    arrive(0)

    def conduct(r, here):
        below = strided(kappa_in, jnp.minimum(r + 1, tall - 1))
        for i in range(count):
            beside = here[i + 1] if i + 1 < count else later(here[0])
            east[r, i] = 0.5 * (here[i] + beside)
            south[r, i] = 0.5 * (here[i] + below[i])
        return below

    lax.fori_loop(0, tall, conduct, strided(kappa_in, 0))
    arrive(1)

    def plain(ref, r):
        return tuple(ref[r, i] for i in range(count))

    for step in range(1, STEPS + 1):
        low = jnp.where(is_first, HALO, step)
        high = jnp.where(is_last, HALO + height, tall - step)
        if step == 1:
            load = functools.partial(strided, field_in)
        else:
            load = functools.partial(plain, field)

        def relax(r, carry, load=load, step=step):
            here, above = carry
            below = load(r + 1)
            down = [south[r, i] * (below[i] - here[i]) for i in range(count)]
            right = []
            for i in range(count):
                beside = here[i + 1] if i + 1 < count else later(here[0])
                right.append(east[r, i] * (beside - here[i]))
            for i in range(count):
                left = right[i - 1] if i > 0 else sooner(right[count - 1])
                new = here[i] + ((right[i] - left) + (down[i] - above[i]))
                if step == STEPS:
                    field_in[r, pl.ds(i, SUB, stride=count), :] = new
                else:
                    field[r, i] = new
            return below, tuple(down)

        before = load(low - 1)
        here = load(low)
        above = tuple(south[low - 1, i] * (here[i] - before[i]) for i in range(count))
        lax.fori_loop(low, high, relax, (here, above))

    result = pltpu.make_async_copy(field_in.at[centre], out_ref, local_sems.at[0])
    result.start()
    for array in range(2):
        for n, (a, b) in enumerate(directions):

            @pl.when(there(a))
            def _(array=array, n=n):
                edge(array, n).wait_send()

    result.wait()


def local(
    lat_count,
    lon_count,
    background,
    diffusivity,
    tile_index,
    anchor,
    weights,
    observed,
    accept,
    absorb,
    sensitivity,
    inverse_variance,
):
    dev_count = lat_count * lon_count
    feet, channels = observed.shape
    cap = max(2, 2 * feet // dev_count)
    height, breadth, levels = background.shape
    slots = dev_count * cap
    width = -(-5 * cap // LANES) * LANES
    shape = jax.ShapeDtypeStruct
    params = functools.partial(pltpu.CompilerParams, vmem_limit_bytes=VMEM_BYTES)
    dma = pltpu.SemaphoreType.DMA

    slot, request = pl.pallas_call(
        functools.partial(request_kernel, cap),
        out_shape=(shape((1, feet), I32), shape((dev_count, 1, width), I32)),
        in_specs=[VMEM_SPEC] * 3,
        out_specs=(VMEM_SPEC, VMEM_SPEC),
        compiler_params=params(),
        name="request",
    )(tile_index.reshape(1, feet), anchor.reshape(1, feet), weights.T)

    asked, arrived = pl.pallas_call(
        functools.partial(columns_kernel, cap, lon_count),
        out_shape=(
            shape((dev_count, 1, width), I32),
            shape((dev_count, cap, levels), F32),
        ),
        in_specs=[VMEM_SPEC] * 2,
        out_specs=(VMEM_SPEC, VMEM_SPEC),
        scratch_shapes=[
            pltpu.VMEM((height * breadth, levels), F32),
            pltpu.VMEM((dev_count, cap, levels), F32),
            pltpu.SMEM((dev_count, 1, width), I32),
            dma((dev_count,)),
            dma((dev_count,)),
            dma((dev_count,)),
            dma((dev_count,)),
            dma,
        ],
        compiler_params=params(collective_id=0, has_side_effects=True),
        name="columns",
    )(request, background.reshape(height * breadth, levels))

    departure, grad = pl.pallas_call(
        assess_kernel,
        out_shape=(shape((feet, channels), F32), shape((slots, levels), F32)),
        in_specs=[VMEM_SPEC] * 7,
        out_specs=(VMEM_SPEC, VMEM_SPEC),
        scratch_shapes=[
            pltpu.VMEM((slots, feet), BF16),
            pltpu.VMEM((feet // LANES, levels, LANES), F32),
            pltpu.VMEM((feet // LANES, levels, LANES), F32),
            pltpu.VMEM((channels, feet), F32),
            pltpu.VMEM((levels, channels, LANES), F32),
            pltpu.VMEM((channels, LANES), F32),
            pltpu.VMEM((channels, LANES), F32),
            pltpu.VMEM((levels, channels, LANES), F32),
            pltpu.VMEM((levels, channels, LANES), F32),
            pltpu.VMEM((2, levels * SUB, LANES), F32),
            pltpu.VMEM((levels, feet), F32),
        ],
        compiler_params=params(),
        name="assess",
    )(
        slot,
        arrived.reshape(slots, levels),
        observed,
        accept,
        absorb,
        sensitivity.reshape(1, channels),
        inverse_variance.reshape(1, channels),
    )

    pulled = pl.pallas_call(
        functools.partial(exchange_kernel, lon_count),
        out_shape=shape((dev_count, cap, levels), F32),
        in_specs=[VMEM_SPEC],
        out_specs=VMEM_SPEC,
        scratch_shapes=[dma((dev_count,)), dma((dev_count,))],
        compiler_params=params(collective_id=1, has_side_effects=True),
        name="exchange",
    )(grad.reshape(dev_count, cap, levels))

    raw = pl.pallas_call(
        functools.partial(spread_kernel, cap),
        out_shape=shape((height * breadth, levels), F32),
        in_specs=[SMEM_SPEC, VMEM_SPEC],
        out_specs=VMEM_SPEC,
        scratch_shapes=[pltpu.VMEM((height * breadth, levels), F32)],
        compiler_params=params(),
        name="spread",
    )(asked, pulled)

    wide = (height + 2 * HALO, breadth + 2 * HALO, levels)
    turned = (height + 2 * HALO, (breadth + 2 * HALO) // SUB, SUB, levels)
    increment = pl.pallas_call(
        functools.partial(diffuse_kernel, lat_count, lon_count),
        out_shape=shape((height, breadth, levels), F32),
        in_specs=[ANY_SPEC, ANY_SPEC],
        out_specs=ANY_SPEC,
        scratch_shapes=[
            pltpu.VMEM(wide, F32),
            pltpu.VMEM(wide, F32),
            pltpu.VMEM(turned, F32),
            pltpu.VMEM(turned, F32),
            pltpu.VMEM(turned, F32),
            dma((2,)),
            dma((2, 8)),
            dma((2, 8)),
        ],
        compiler_params=params(collective_id=2, has_side_effects=True),
        name="diffuse",
    )(raw.reshape(height, breadth, levels), diffusivity)
    return (departure, increment)


def solution(mesh):
    in_specs = (
        P("lat", "lon", None),
        P("lat", "lon", None),
        P(("lat", "lon"), None),
        P(("lat", "lon")),
        P(("lat", "lon"), None),
        P(("lat", "lon"), None),
        P(("lat", "lon"), None),
        P(),
        P(),
        P(),
    )
    out_specs = (P(("lat", "lon"), None), P("lat", "lon", None))
    return jax.shard_map(
        functools.partial(local, mesh.shape["lat"], mesh.shape["lon"]),
        mesh=mesh,
        in_specs=in_specs,
        out_specs=out_specs,
        check_vma=False,
    )
```

time: 481 us -> 142 us (0.30); the launches traced: 473 us -> 142 us
  other arithmetic: 306 us -> 0 us
  Pallas kernels: 0 us -> 138 us
  starting transfers between devices: 82 us -> 0 us
  waiting for transfers between devices: 42.8 us -> 0 us
  local copies, waits for them, and re-layouts: 39.4 us -> 3.16 us
    another operation x22 -> x0, other arithmetic: 166 us -> none  [the longest x16 166 us: evolve(): optical = jnp.cumsum(layer_depth, axis=1)]
    pallas_call x0 -> x6, Pallas kernels: none -> 138 us  [the longest x1 38.8 us: local(): pl.pallas_call(functools.partial(columns_kernel, cap, lon_count), out_sha...]
    ppermute x20 -> x0, starting transfers between devices: 52.8 us -> none  [the longest x10 36.3 us: padded_2(): lax.ppermute(lax.slice_in_dim(block, 0, width, axis=dim), axis, backward)]
    reduce_sum x27 -> x0, other arithmetic: 45.7 us -> none  [the longest x16 33.4 us: evolve(): layered = jnp.sum(profile[:, :, None] * (transmit_above - transmit), axis=1)]
    all_to_all x4 -> x0, starting transfers between devices: 29.3 us -> none  [the longest x1 11.5 us: local(): lax.all_to_all(request, ('lat', 'lon'), split_axis=0, concat_axis=0, tile...]
    mul x12 -> x0, other arithmetic: 28.5 us -> none  [the longest x4 21.6 us: local(): middle = relax(extend(grid_field, 2), kappa_ext) * inside]
    all_to_all x4 -> x0, waiting for transfers between devices: 26.4 us -> none  [the longest x1 14.1 us: local(): lax.all_to_all(local_profiles, ('lat', 'lon'), split_axis=0, concat_axis=...]
    scatter-add x1 -> x0, other arithmetic: 26.3 us -> none  [local(): increment = jnp.zeros((tile_rows * tile_cols, levels), jnp.float32).at[as...]
  transfers between devices with their start and end apart: 24 -> 0, of which waited for: 11 -> 0; matrix products, arithmetic and copies ran while one was open for 5% -> 0% of each run, Pallas kernels for 0% -> 0%
where the time goes in v1:
time: 142 us
  Pallas kernels  138 us (97%)
  local copies, waits for them, and re-layouts  3.16 us (2%)
    pallas_call x1, Pallas kernels, local(): pl.pallas_call(functools.partial(columns_kernel, cap, lon_count), out_sha...  38.8 us
    pallas_call x1, Pallas kernels, local(): pl.pallas_call(assess_kernel, out_shape=(shape((feet, channels), F32), sh...  35.6 us
    pallas_call x1, Pallas kernels, local(): pl.pallas_call(functools.partial(diffuse_kernel, lat_count, lon_count), o...  31.3 us
    pallas_call x1, Pallas kernels, local(): pl.pallas_call(functools.partial(exchange_kernel, lon_count), out_shape=s...  21.3 us
    pallas_call x1, Pallas kernels, local(): pl.pallas_call(functools.partial(spread_kernel, cap), out_shape=shape((he...  8.69 us
    unnamed x1, local copies, waits for them, and re-layouts  3.16 us

profile of v1, /device:TPU:1, one launch (start us, length us, event | category | flops | bytes accessed | tf_op | source)
XLA Modules:
  0.0 141.5 jit_solution(12629856041551269436)
XLA Ops:
  0.6 2.0 %request.1 = (s32[1,512]{1,0:T(1,128)}, s32[128,1,128]{2,1,0:T(1,128)}) custom-call(s32[1,512]{1,0:T(1,128)} %bitcast.14, s32[1,512]{1,0:T(1,128)} %bitcast.15, f32[4,512]{1,0:T(4,128)} %bitcast.13), custom_call_target="tpu_custom_call" | custom-call | tf_op jit(solution)/shard_map/request/pallas_call | solution.py:606
  2.6 38.8 %columns.1 = (s32[128,1,128]{2,1,0:T(1,128)}, f32[128,8,128]{2,1,0:T(8,128)}) custom-call(s32[128,1,128]{2,1,0:T(1,128)} %get-tuple-element.9.request_ref, bf16[4096,128]{1,0:T(8,128)(2,1)} %bitcast.10), custom_call_target="tpu_custom_call" | custom-call | tf_op jit(solution)/shard_map/columns/pallas_call | solution.py:615
  41.4 35.6 %assess.1 = (f32[512,128]{1,0:T(8,128)}, f32[1024,128]{1,0:T(8,128)}) custom-call(s32[1,512]{1,0:T(1,128)} %get-tuple-element.8.slot_ref, f32[1024,128]{1,0:T(8,128)} %bitcast.11, f32[512,128]{1,0:T(8,128)} %observed_ref.1, s32[512,128]{1,0:T(8,128)} %accept_ref.1, f32[128,128]{1,0:T(8,128)} %absorb_ref.1, f32[1,128]{1,0:T(1,128)} %bitcast.16, f32[1,128]{1,0:T(1,128)} %bitcast.17), custom_call_target="tpu_custom_call" | custom-call | tf_op jit(solution)/shard_map/assess/pallas_call | solution.py:637
  77.1 21.3 %exchange.1.arrived_ref = f32[128,8,128]{2,1,0:T(8,128)} custom-call(f32[128,8,128]{2,1,0:T(8,128)} %bitcast.12), custom_call_target="tpu_custom_call" | custom-call | tf_op jit(solution)/shard_map/exchange/pallas_call | solution.py:667
  98.3 8.7 %spread.1 = f32[4096,128]{1,0:T(8,128)} custom-call(s32[128,1,128]{2,1,0:T(1,128)} %get-tuple-element.12.asked_ref, f32[128,8,128]{2,1,0:T(8,128)} %exchange.1.arrived_ref), custom_call_target="tpu_custom_call" | custom-call | tf_op jit(solution)/shard_map/spread/pallas_call | solution.py:677
  107.0 31.3 %diffuse.1 = f32[64,64,128]{2,1,0:T(8,128)} custom-call(f32[64,64,128]{2,1,0:T(8,128)} %bitcast.9, f32[64,64,128]{2,1,0:T(8,128)} %kappa_ref.1), custom_call_target="tpu_custom_call" | custom-call | tf_op jit(solution)/shard_map/diffuse/pallas_call | solution.py:689
  138.4 3.2 %copy.13 = f32[64,64,128]{2,1,0:T(8,128)} copy(f32[64,64,128]{2,1,0:T(8,128)} %diffuse.1) | data formatting | bytes 4194304

commit v2 on v1

--- a/solution.py
+++ b/solution.py
@@ -89,165 +89,105 @@
     return barrier
 
 
-def columns_kernel(
-    cap,
-    lon_count,
-    request_ref,
-    background_ref,
-    asked_ref,
-    profile_ref,
-    field,
-    found,
-    asked_smem,
-    ask_send,
-    ask_recv,
-    back_send,
-    back_recv,
-    local_sem,
-):
-    dev_count = request_ref.shape[0]
-    me = my_index(lon_count)
-    tile_cols = 64
-    barrier = greet_all(me, dev_count, lon_count)
-
-    chunk = 256
-
-    @pl.loop(0, background_ref.shape[0] // chunk)
-    def _(j):
-        at = pl.ds(pl.multiple_of(j * chunk, chunk), chunk)
-        field[at, :] = background_ref[at, :].astype(F32)
-
-    pl.semaphore_wait(barrier, dev_count - 1)
-
-    def ask(other):
-        return pltpu.make_async_remote_copy(
-            src_ref=request_ref.at[other],
-            dst_ref=asked_ref.at[me],
-            send_sem=ask_send.at[other],
-            recv_sem=ask_recv.at[me],
-            device_id=coordinates(other, lon_count),
-            device_id_type=MESH,
-        )
-
-    def ask_from(other):
-        return pltpu.make_async_remote_copy(
-            src_ref=request_ref.at[other],
-            dst_ref=asked_ref.at[other],
-            send_sem=ask_send.at[other],
-            recv_sem=ask_recv.at[other],
-            device_id=coordinates(other, lon_count),
-            device_id_type=MESH,
-        )
-
-    @pl.loop(1, dev_count)
-    def _(d):
-        ask(lax.rem(me + d, dev_count)).start()
-
-    asked_ref[me] = request_ref[me]
-
-    @pl.loop(1, dev_count)
-    def _(d):
-        ask_from(lax.rem(me + d, dev_count)).wait_recv()
-
-    to_smem = pltpu.make_async_copy(asked_ref, asked_smem, local_sem)
-    to_smem.start()
-    to_smem.wait()
-
-    def gather(source):
-        for r in range(cap):
-            at = asked_smem[source, 0, r]
-            total = None
-            for k, offset in enumerate((0, 1, tile_cols, tile_cols + 1)):
-                share = asked_smem[source, 0, (k + 1) * cap + r].astype(F32)
-                term = share * field[pl.ds(at + offset, 1), :]
-                total = term if total is None else total + term
-            found[source, r : r + 1, :] = total * (1.0 / FIXED)
-
-    def back(source):
-        return pltpu.make_async_remote_copy(
-            src_ref=found.at[source],
-            dst_ref=profile_ref.at[me],
-            send_sem=back_send.at[source],
-            recv_sem=back_recv.at[me],
-            device_id=coordinates(source, lon_count),
-            device_id_type=MESH,
-        )
-
-    def back_from(other):
-        return pltpu.make_async_remote_copy(
-            src_ref=found.at[other],
-            dst_ref=profile_ref.at[other],
-            send_sem=back_send.at[other],
-            recv_sem=back_recv.at[other],
-            device_id=coordinates(other, lon_count),
-            device_id_type=MESH,
-        )
-
-    @pl.loop(1, dev_count)
-    def _(d):
-        source = lax.rem(me + d, dev_count)
-        gather(source)
-        back(source).start()
-
-    gather(me)
-    profile_ref[me] = found[me]
+def all_of(ref, sem):
+    blocks = ref.at[pl.ds(0, ref.shape[0] - 1)]
+    pltpu.make_async_copy(blocks, blocks, sem).wait()
+
+
+def scatter_blocks(me, lon_count, given, taken, send, recv, before=None):
+    dev_count = given.shape[0]
 
     @pl.loop(1, dev_count)
     def _(d):
         other = lax.rem(me + d, dev_count)
-        ask(other).wait_send()
-        back(other).wait_send()
-        back_from(other).wait_recv()
-
-
-def exchange_kernel(lon_count, given_ref, taken_ref, send, recv):
-    dev_count = given_ref.shape[0]
-    me = my_index(lon_count)
-    barrier = greet_all(me, dev_count, lon_count)
-    taken_ref[me] = given_ref[me]
-    pl.semaphore_wait(barrier, dev_count - 1)
-
-    def give(other):
-        return pltpu.make_async_remote_copy(
-            src_ref=given_ref.at[other],
-            dst_ref=taken_ref.at[me],
-            send_sem=send.at[other],
-            recv_sem=recv.at[me],
+        if before is not None:
+            before(other)
+        pltpu.make_async_remote_copy(
+            src_ref=given.at[other],
+            dst_ref=taken.at[me],
+            send_sem=send,
+            recv_sem=recv,
             device_id=coordinates(other, lon_count),
             device_id_type=MESH,
-        )
-
-    def take(other):
+        ).start()
+
+    if before is not None:
+        before(me)
+    taken[me] = given[me]
+
+
+DIRECTIONS = [(a, b) for a in (-1, 0, 1) for b in (-1, 0, 1) if (a, b) != (0, 0)]
+
+
+class Edges:
+    def __init__(self, lat_count, lon_count, source, target, send, recv):
+        self.lat_count, self.lon_count = lat_count, lon_count
+        self.source, self.target, self.send, self.recv = source, target, send, recv
+        self.lat, self.lon = lax.axis_index("lat"), lax.axis_index("lon")
+
+    def there(self, a):
+        return jnp.logical_and(self.lat + a >= 0, self.lat + a < self.lat_count)
+
+    def device(self, a, b):
+        return (self.lat + a, lax.rem(self.lon + b + self.lon_count, self.lon_count))
+
+    def copy(self, n):
+        def span(step, size):
+            given = {-1: pl.ds(0, HALO), 0: pl.ds(0, size), 1: pl.ds(size - HALO, HALO)}[step]
+            taken = {-1: pl.ds(HALO + size, HALO), 0: pl.ds(HALO, size), 1: pl.ds(0, HALO)}[step]
+            return given, taken
+
+        a, b = DIRECTIONS[n]
+        given_rows, taken_rows = span(a, self.source.shape[0])
+        given_cols, taken_cols = span(b, self.source.shape[1])
         return pltpu.make_async_remote_copy(
-            src_ref=given_ref.at[other],
-            dst_ref=taken_ref.at[other],
-            send_sem=send.at[other],
-            recv_sem=recv.at[other],
-            device_id=coordinates(other, lon_count),
+            src_ref=self.source.at[given_rows, given_cols],
+            dst_ref=self.target.at[taken_rows, taken_cols],
+            send_sem=self.send.at[n],
+            recv_sem=self.recv.at[n],
+            device_id=self.device(a, b),
             device_id_type=MESH,
         )
 
-    @pl.loop(1, dev_count)
-    def _(d):
-        give(lax.rem(me + d, dev_count)).start()
-
-    @pl.loop(1, dev_count)
-    def _(d):
-        other = lax.rem(me + d, dev_count)
-        give(other).wait_send()
-        take(other).wait_recv()
-
-
-def assess_kernel(
+    def each(self, sign, act):
+        for n, (a, b) in enumerate(DIRECTIONS):
+
+            @pl.when(self.there(sign * a))
+            def _(n=n):
+                act(self.copy(n))
+
+    def start(self):
+        self.each(1, lambda copy: copy.start())
+
+    def arrive(self):
+        self.each(-1, lambda copy: copy.wait_recv())
+
+    def sent(self):
+        self.each(1, lambda copy: copy.wait_send())
+
+
+def observe_kernel(
+    cap,
+    lat_count,
+    lon_count,
     slot_ref,
-    arrived_ref,
+    request_ref,
+    background_ref,
     observed_ref,
     accept_ref,
     absorb_ref,
     sensitivity_ref,
     variance_ref,
+    kappa_ref,
+    asked_ref,
     departure_ref,
-    grad_ref,
+    pulled_ref,
+    kappa_wide_ref,
+    field,
+    found,
+    arrived,
+    asked_smem,
+    zeros,
     chosen,
     profile,
     slope,
@@ -259,8 +199,44 @@
     transmit,
     sums,
     adjoint,
+    block_send,
+    block_recv,
+    edge_send,
+    edge_recv,
+    local_sems,
 ):
-    slots, levels = arrived_ref.shape
+    dev_count = request_ref.shape[0]
+    tile_cols = 64
+    me = my_index(lon_count)
+    barrier = greet_all(me, dev_count, lon_count)
+
+    height, breadth, levels = kappa_ref.shape
+    edges = Edges(lat_count, lon_count, kappa_ref, kappa_wide_ref, edge_send, edge_recv)
+    own = pltpu.make_async_copy(
+        kappa_ref, kappa_wide_ref.at[pl.ds(HALO, height), pl.ds(HALO, breadth)], local_sems.at[0]
+    )
+    own.start()
+    zeros[...] = jnp.zeros(zeros.shape, F32)
+
+    def blank(a):
+        rows = pl.ds(0, HALO) if a < 0 else pl.ds(HALO + height, HALO)
+        return pltpu.make_async_copy(zeros, kappa_wide_ref.at[rows], local_sems.at[1])
+
+    for a in (-1, 1):
+
+        @pl.when(jnp.logical_not(edges.there(a)))
+        def _(a=a):
+            blank(a).start()
+            blank(a).wait()
+
+    chunk = 256
+
+    @pl.loop(0, background_ref.shape[0] // chunk)
+    def _(j):
+        at = pl.ds(pl.multiple_of(j * chunk, chunk), chunk)
+        field[at, :] = background_ref[at, :].astype(F32)
+
+    slots = dev_count * cap
     feet, channels = observed_ref.shape
     groups = feet // LANES
     parts = channels // SUB
@@ -278,6 +254,12 @@
         for i in range(SUB):
             absorb_wide[j * SUB + i] = jnp.broadcast_to(turned[:, i : i + 1], (channels, LANES))
 
+    pl.semaphore_wait(barrier, dev_count - 1)
+    scatter_blocks(
+        me, lon_count, request_ref, asked_ref, block_send.at[0], block_recv.at[0]
+    )
+    edges.start()
+
     block = 256 if slots % 256 == 0 else slots
 
     @pl.loop(0, slots // block)
@@ -286,7 +268,40 @@
         here = lax.broadcasted_iota(I32, (block, feet), 0) + first == slot_ref[...]
         chosen[pl.ds(first, block), :] = here.astype(F32).astype(BF16)
 
-    arrived_t = jnp.swapaxes(arrived_ref[...], 0, 1)
+    for g in range(groups):
+        at = pl.ds(g * LANES, LANES)
+        accepted = accept_ref[at, :].astype(F32) * variance_ref[...]
+        weight[:, at] = jnp.swapaxes(accepted, 0, 1)
+
+    level = lax.broadcasted_iota(I32, (levels, levels * SUB), 0)
+    source = lax.broadcasted_iota(I32, (levels, levels * SUB), 1) // SUB
+    same = (level == source).astype(F32)
+    fall = (level == source + 1).astype(F32) - jnp.where(level == levels - 1, 0.0, same)
+    same = same.astype(BF16)
+    fall = fall.astype(BF16)
+
+    all_of(asked_ref, block_recv.at[0])
+    to_smem = pltpu.make_async_copy(asked_ref, asked_smem, local_sems.at[1])
+    to_smem.start()
+    to_smem.wait()
+
+    def gather(source):
+        for r in range(cap):
+            at = asked_smem[source, 0, r]
+            total = None
+            for k, offset in enumerate((0, 1, tile_cols, tile_cols + 1)):
+                share = asked_smem[source, 0, (k + 1) * cap + r].astype(F32)
+                term = share * field[pl.ds(at + offset, 1), :]
+                total = term if total is None else total + term
+            found[source, r : r + 1, :] = total * (1.0 / FIXED)
+
+    scatter_blocks(
+        me, lon_count, found, arrived, block_send.at[1], block_recv.at[1], gather
+    )
+    all_of(arrived, block_recv.at[1])
+    all_of(found, block_send.at[1])
+
+    arrived_t = jnp.swapaxes(arrived[...].reshape(slots, levels), 0, 1)
     high, middle, low = pieces(arrived_t)
     plain = ((1,), (0,))
     mine = dot(high, chosen[...], plain) + dot(middle, chosen[...], plain) + dot(low, chosen[...], plain)
@@ -295,18 +310,6 @@
         at = slice(g * LANES, (g + 1) * LANES)
         profile[g] = mine[:, at]
         slope[g] = below[:, at] - mine[:, at]
-
-    for g in range(groups):
-        at = pl.ds(g * LANES, LANES)
-        accepted = accept_ref[at, :].astype(F32) * variance_ref[...]
-        weight[:, at] = jnp.swapaxes(accepted, 0, 1)
-
-    level = lax.broadcasted_iota(I32, (levels, levels * SUB), 0)
-    source = lax.broadcasted_iota(I32, (levels, levels * SUB), 1) // SUB
-    same = (level == source).astype(F32)
-    fall = (level == source + 1).astype(F32) - jnp.where(level == levels - 1, 0.0, same)
-    same = same.astype(BF16)
-    fall = fall.astype(BF16)
 
     for g in range(groups):
         at = pl.ds(g * LANES, LANES)
@@ -327,7 +330,7 @@
             return tuple(out)
 
         zero = jnp.zeros((SUB, LANES), F32)
-        done = lax.fori_loop(0, levels, descend, ((zero, zero),) * parts, unroll=2)
+        done = lax.fori_loop(0, levels, descend, ((zero, zero),) * parts, unroll=4)
         top = profile[g, 0:1, :]
         observed_t = jnp.swapaxes(observed_ref[at, :], 0, 1)
         departed = []
@@ -363,7 +366,7 @@
             sums[1, at_l, :] = layer_sum
             return tuple(out)
 
-        lax.fori_loop(0, levels, ascend, (zero,) * parts, unroll=2)
+        lax.fori_loop(0, levels, ascend, (zero,) * parts, unroll=4)
         total = None
         for matrix, index in ((fall, 0), (same, 1)):
             for piece in pieces(sums[index]):
@@ -381,7 +384,18 @@
         for piece in parts_adjoint:
             term = dot(chosen[rows, :], piece, ((1,), (1,)))
             total = term if total is None else total + term
-        grad_ref[rows, :] = total
+        found[pl.ds(pl.multiple_of(j * (block // cap), block // cap), block // cap)] = total.reshape(
+            block // cap, cap, levels
+        )
+
+
+    scatter_blocks(me, lon_count, found, pulled_ref, block_send.at[2], block_recv.at[2])
+    own.wait()
+    edges.sent()
+    edges.arrive()
+    all_of(request_ref, block_send.at[0])
+    all_of(found, block_send.at[2])
+    all_of(pulled_ref, block_recv.at[2])
 
 
 def spread_kernel(cap, asked_ref, arrived_ref, raw_ref, other):
@@ -433,84 +447,42 @@
     height, breadth, levels = raw_ref.shape
     tall = height + 2 * HALO
     count = (breadth + 2 * HALO) // SUB
-    lat = lax.axis_index("lat")
-    lon = lax.axis_index("lon")
-    is_first = lat == 0
-    is_last = lat == lat_count - 1
-
-    directions = [(a, b) for a in (-1, 0, 1) for b in (-1, 0, 1) if (a, b) != (0, 0)]
-
-    def there(a):
-        return jnp.logical_and(lat + a >= 0, lat + a < lat_count)
-
-    def device(a, b):
-        return (lat + a, lax.rem(lon + b + lon_count, lon_count))
+    edges = Edges(lat_count, lon_count, raw_ref, field_in, send_sems, recv_sems)
+    is_first = edges.lat == 0
+    is_last = edges.lat == lat_count - 1
 
     barrier = pltpu.get_barrier_semaphore()
-    for a, b in directions:
-
-        @pl.when(there(a))
+    for a, b in DIRECTIONS:
+
+        @pl.when(edges.there(a))
         def _(a=a, b=b):
-            pl.semaphore_signal(barrier, inc=1, device_id=device(a, b), device_id_type=MESH)
-
-    own = []
+            pl.semaphore_signal(
+                barrier, inc=1, device_id=edges.device(a, b), device_id_type=MESH
+            )
+
     centre = (pl.ds(HALO, height), pl.ds(HALO, breadth))
-    for n, (source, target) in enumerate(((kappa_ref, kappa_in), (raw_ref, field_in))):
-        copy = pltpu.make_async_copy(source, target.at[centre], local_sems.at[n])
-        copy.start()
-        own.append(copy)
+    kappa_copy = pltpu.make_async_copy(kappa_ref, kappa_in, local_sems.at[0])
+    kappa_copy.start()
+    own = pltpu.make_async_copy(raw_ref, field_in.at[centre], local_sems.at[1])
+    own.start()
 
     zero_rows = jnp.zeros((HALO, breadth + 2 * HALO, levels), F32)
     flat_rows = jnp.zeros((HALO, count, SUB, levels), F32)
 
     @pl.when(is_first)
     def _():
-        kappa_in[pl.ds(0, HALO)] = zero_rows
         field_in[pl.ds(0, HALO)] = zero_rows
         field[pl.ds(0, HALO)] = flat_rows
 
     @pl.when(is_last)
     def _():
-        kappa_in[pl.ds(HALO + height, HALO)] = zero_rows
         field_in[pl.ds(HALO + height, HALO)] = zero_rows
         field[pl.ds(HALO + height, HALO)] = flat_rows
 
     neighbours = 8 - 3 * is_first.astype(I32) - 3 * is_last.astype(I32)
     pl.semaphore_wait(barrier, neighbours)
-
-    def span(step, size):
-        given = {-1: pl.ds(0, HALO), 0: pl.ds(0, size), 1: pl.ds(size - HALO, HALO)}[step]
-        taken = {-1: pl.ds(HALO + size, HALO), 0: pl.ds(HALO, size), 1: pl.ds(0, HALO)}[step]
-        return given, taken
-
-    def edge(array, n):
-        a, b = directions[n]
-        source, target = ((kappa_ref, kappa_in), (raw_ref, field_in))[array]
-        given_rows, taken_rows = span(a, height)
-        given_cols, taken_cols = span(b, breadth)
-        return pltpu.make_async_remote_copy(
-            src_ref=source.at[given_rows, given_cols],
-            dst_ref=target.at[taken_rows, taken_cols],
-            send_sem=send_sems.at[array, n],
-            recv_sem=recv_sems.at[array, n],
-            device_id=device(a, b),
-            device_id_type=MESH,
-        )
-
-    for array in range(2):
-        for n, (a, b) in enumerate(directions):
-
-            @pl.when(there(a))
-            def _(array=array, n=n):
-                edge(array, n).start()
-
-    def arrive(array):
-        own[array].wait()
-        for n, (a, b) in enumerate(directions):
-
-            @pl.when(there(-a))
-            def _(n=n):
-                edge(array, n).wait_recv()
+    edges.start()
+    kappa_copy.wait()
 
     def strided(ref, r):
         return tuple(ref[r, pl.ds(i, SUB, stride=count), :] for i in range(count))
@@ -520,8 +492,6 @@
 
     def sooner(x):
         return pltpu.roll(x, 1, 0)
-
-    arrive(0)
 
     def conduct(r, here):
         below = strided(kappa_in, jnp.minimum(r + 1, tall - 1))
@@ -532,7 +502,8 @@
         return below
 
     lax.fori_loop(0, tall, conduct, strided(kappa_in, 0))
-    arrive(1)
+    own.wait()
+    edges.arrive()
 
     def plain(ref, r):
         return tuple(ref[r, i] for i in range(count))
@@ -569,13 +540,7 @@
 
     result = pltpu.make_async_copy(field_in.at[centre], out_ref, local_sems.at[0])
     result.start()
-    for array in range(2):
-        for n, (a, b) in enumerate(directions):
-
-            @pl.when(there(a))
-            def _(array=array, n=n):
-                edge(array, n).wait_send()
-
+    edges.sent()
     result.wait()
 
 
@@ -612,34 +577,23 @@
         name="request",
     )(tile_index.reshape(1, feet), anchor.reshape(1, feet), weights.T)
 
-    asked, arrived = pl.pallas_call(
-        functools.partial(columns_kernel, cap, lon_count),
+    wide = (height + 2 * HALO, breadth + 2 * HALO, levels)
+    asked, departure, pulled, kappa_wide = pl.pallas_call(
+        functools.partial(observe_kernel, cap, lat_count, lon_count),
         out_shape=(
             shape((dev_count, 1, width), I32),
+            shape((feet, channels), F32),
             shape((dev_count, cap, levels), F32),
+            shape(wide, F32),
         ),
-        in_specs=[VMEM_SPEC] * 2,
-        out_specs=(VMEM_SPEC, VMEM_SPEC),
+        in_specs=[VMEM_SPEC] * 8 + [ANY_SPEC],
+        out_specs=(VMEM_SPEC, VMEM_SPEC, VMEM_SPEC, ANY_SPEC),
         scratch_shapes=[
             pltpu.VMEM((height * breadth, levels), F32),
             pltpu.VMEM((dev_count, cap, levels), F32),
+            pltpu.VMEM((dev_count, cap, levels), F32),
             pltpu.SMEM((dev_count, 1, width), I32),
-            dma((dev_count,)),
-            dma((dev_count,)),
-            dma((dev_count,)),
-            dma((dev_count,)),
-            dma,
-        ],
-        compiler_params=params(collective_id=0, has_side_effects=True),
-        name="columns",
-    )(request, background.reshape(height * breadth, levels))
-
-    departure, grad = pl.pallas_call(
-        assess_kernel,
-        out_shape=(shape((feet, channels), F32), shape((slots, levels), F32)),
-        in_specs=[VMEM_SPEC] * 7,
-        out_specs=(VMEM_SPEC, VMEM_SPEC),
-        scratch_shapes=[
+            pltpu.VMEM((HALO,) + wide[1:], F32),
             pltpu.VMEM((slots, feet), BF16),
             pltpu.VMEM((feet // LANES, levels, LANES), F32),
             pltpu.VMEM((feet // LANES, levels, LANES), F32),
@@ -651,28 +605,25 @@
             pltpu.VMEM((levels, channels, LANES), F32),
             pltpu.VMEM((2, levels * SUB, LANES), F32),
             pltpu.VMEM((levels, feet), F32),
+            dma((3,)),
+            dma((3,)),
+            dma((8,)),
+            dma((8,)),
+            dma((2,)),
         ],
-        compiler_params=params(),
-        name="assess",
+        compiler_params=params(collective_id=0, has_side_effects=True),
+        name="observe",
     )(
         slot,
-        arrived.reshape(slots, levels),
+        request,
+        background.reshape(height * breadth, levels),
         observed,
         accept,
         absorb,
         sensitivity.reshape(1, channels),
         inverse_variance.reshape(1, channels),
-    )
-
-    pulled = pl.pallas_call(
-        functools.partial(exchange_kernel, lon_count),
-        out_shape=shape((dev_count, cap, levels), F32),
-        in_specs=[VMEM_SPEC],
-        out_specs=VMEM_SPEC,
-        scratch_shapes=[dma((dev_count,)), dma((dev_count,))],
-        compiler_params=params(collective_id=1, has_side_effects=True),
-        name="exchange",
-    )(grad.reshape(dev_count, cap, levels))
+        diffusivity,
+    )
 
     raw = pl.pallas_call(
         functools.partial(spread_kernel, cap),
@@ -684,7 +635,6 @@
         name="spread",
     )(asked, pulled)
 
-    wide = (height + 2 * HALO, breadth + 2 * HALO, levels)
     turned = (height + 2 * HALO, (breadth + 2 * HALO) // SUB, SUB, levels)
     increment = pl.pallas_call(
         functools.partial(diffuse_kernel, lat_count, lon_count),
@@ -698,12 +648,12 @@
             pltpu.VMEM(turned, F32),
             pltpu.VMEM(turned, F32),
             dma((2,)),
-            dma((2, 8)),
-            dma((2, 8)),
+            dma((8,)),
+            dma((8,)),
         ],
-        compiler_params=params(collective_id=2, has_side_effects=True),
+        compiler_params=params(collective_id=1, has_side_effects=True),
         name="diffuse",
-    )(raw.reshape(height, breadth, levels), diffusivity)
+    )(raw.reshape(height, breadth, levels), kappa_wide)
     return (departure, increment)
 
 

time: 142 us -> 112 us (0.79)
  Pallas kernels: 138 us -> 108 us
    pallas_call x3 -> x1, Pallas kernels: 95.7 us -> 71 us  [local(): pl.pallas_call(functools.partial(observe_kernel, cap, lat_count, lon_coun...]
    pallas_call x1, Pallas kernels: 31.3 us -> 25.9 us  [local(): pl.pallas_call(functools.partial(diffuse_kernel, lat_count, lon_count), o...]
    unnamed x1 -> x4, local copies, waits for them, and re-layouts: 3.16 us -> 3.87 us
where the time goes in v2:
time: 112 us
  Pallas kernels  108 us (96%)
  local copies, waits for them, and re-layouts  3.87 us (3%)
    pallas_call x1, Pallas kernels, local(): pl.pallas_call(functools.partial(observe_kernel, cap, lat_count, lon_coun...  71 us
    pallas_call x1, Pallas kernels, local(): pl.pallas_call(functools.partial(diffuse_kernel, lat_count, lon_count), o...  25.9 us
    pallas_call x1, Pallas kernels, local(): pl.pallas_call(functools.partial(spread_kernel, cap), out_shape=shape((he...  8.69 us
    unnamed x4, local copies, waits for them, and re-layouts  3.87 us

profile of v2, /device:TPU:1, one launch (start us, length us, event | category | flops | bytes accessed | tf_op | source)
XLA Modules:
  0.0 112.1 jit_solution(15359644150022691831)
XLA Ops:
  0.6 2.0 %request.1 = (s32[1,512]{1,0:T(1,128)}, s32[128,1,128]{2,1,0:T(1,128)}) custom-call(s32[1,512]{1,0:T(1,128)} %bitcast.10, s32[1,512]{1,0:T(1,128)} %bitcast.11, f32[4,512]{1,0:T(4,128)} %bitcast.9), custom_call_target="tpu_custom_call" | custom-call | tf_op jit(solution)/shard_map/request/pallas_call | solution.py:571
  2.6 71.0 %observe.1 = (s32[128,1,128]{2,1,0:T(1,128)}, f32[512,128]{1,0:T(8,128)}, f32[128,8,128]{2,1,0:T(8,128)}, f32[80,80,128]{2,1,0:T(8,128)}) custom-call(s32[1,512]{1,0:T(1,128)} %get-tuple-element.8.slot_ref, s32[128,1,128]{2,1,0:T(1,128)} %get-tuple-element.9.request_ref, bf16[4096,128]{1,0:T(8,128)(2,1)} %bitcast.8, f32[512,128]{1,0:T(8,128)} %observed_ref.1, ...), custom_call_target="tpu_custom_call" | custom-call | tf_op jit(solution)/shard_map/observe/pallas_call | solution.py:581
  73.6 8.7 %spread.1 = f32[4096,128]{1,0:T(8,128)} custom-call(s32[128,1,128]{2,1,0:T(1,128)} %get-tuple-element.11.asked_ref, f32[128,8,128]{2,1,0:T(8,128)} %get-tuple-element.12.arrived_ref), custom_call_target="tpu_custom_call" | custom-call | tf_op jit(solution)/shard_map/spread/pallas_call | solution.py:628
  82.3 0.0 copy-start
  82.3 25.9 %diffuse.1 = f32[64,64,128]{2,1,0:T(8,128)} custom-call(f32[64,64,128]{2,1,0:T(8,128)} %bitcast.7, f32[80,80,128]{2,1,0:T(8,128)} %get-tuple-element.13.kappa_ref), custom_call_target="tpu_custom_call" | custom-call | tf_op jit(solution)/shard_map/diffuse/pallas_call | solution.py:639
  108.2 0.0 copy-done
  108.2 0.7 copy.14
  108.9 3.2 %copy.15 = f32[64,64,128]{2,1,0:T(8,128)} copy(f32[64,64,128]{2,1,0:T(8,128)} %diffuse.1) | data formatting | bytes 4194304
Async XLA Ops:
  82.3 25.9 %copy-start = (f32[512,128]{1,0:T(8,128)S(1)}, f32[512,128]{1,0:T(8,128)}, u32[]{:S(2)}) copy-start(f32[512,128]{1,0:T(8,128)} %get-tuple-element.16) | copy-start | bytes 786436

commit v3 on v2

--- a/solution.py
+++ b/solution.py
@@ -21,7 +21,7 @@
 VMEM_SPEC = pl.BlockSpec(memory_space=pltpu.VMEM)
 SMEM_SPEC = pl.BlockSpec(memory_space=pltpu.SMEM)
 ANY_SPEC = pl.BlockSpec(memory_space=pl.ANY)
-VMEM_BYTES = 56 * 2**20
+VMEM_BYTES = 60 * 2**20
 
 
 def pieces(x):
@@ -120,9 +120,10 @@
 
 
 class Edges:
-    def __init__(self, lat_count, lon_count, source, target, send, recv):
+    def __init__(self, lat_count, lon_count, source, target, send, recv, size=None):
         self.lat_count, self.lon_count = lat_count, lon_count
         self.source, self.target, self.send, self.recv = source, target, send, recv
+        self.size = source.shape[:2] if size is None else size
         self.lat, self.lon = lax.axis_index("lat"), lax.axis_index("lon")
 
     def there(self, a):
@@ -131,15 +132,18 @@
     def device(self, a, b):
         return (self.lat + a, lax.rem(self.lon + b + self.lon_count, self.lon_count))
 
-    def copy(self, n):
+    def copy(self, n, band=None):
         def span(step, size):
             given = {-1: pl.ds(0, HALO), 0: pl.ds(0, size), 1: pl.ds(size - HALO, HALO)}[step]
             taken = {-1: pl.ds(HALO + size, HALO), 0: pl.ds(HALO, size), 1: pl.ds(0, HALO)}[step]
             return given, taken
 
         a, b = DIRECTIONS[n]
-        given_rows, taken_rows = span(a, self.source.shape[0])
-        given_cols, taken_cols = span(b, self.source.shape[1])
+        given_rows, taken_rows = span(a, self.size[0])
+        given_cols, taken_cols = span(b, self.size[1])
+        if band is not None:
+            given_rows = pl.ds(band * HALO, HALO)
+            taken_rows = pl.ds(HALO + band * HALO, HALO)
         return pltpu.make_async_remote_copy(
             src_ref=self.source.at[given_rows, given_cols],
             dst_ref=self.target.at[taken_rows, taken_cols],
@@ -149,15 +153,17 @@
             device_id_type=MESH,
         )
 
-    def each(self, sign, act):
+    def each(self, sign, act, which=lambda a: True):
         for n, (a, b) in enumerate(DIRECTIONS):
+            if not which(a):
+                continue
 
             @pl.when(self.there(sign * a))
             def _(n=n):
                 act(self.copy(n))
 
-    def start(self):
-        self.each(1, lambda copy: copy.start())
+    def start(self, which=lambda a: True):
+        self.each(1, lambda copy: copy.start(), which)
 
     def arrive(self):
         self.each(-1, lambda copy: copy.wait_recv())
@@ -179,15 +185,14 @@
     sensitivity_ref,
     variance_ref,
     kappa_ref,
+    departure_ref,
+    increment_ref,
     asked_ref,
-    departure_ref,
     pulled_ref,
-    kappa_wide_ref,
-    field,
+    columns,
     found,
     arrived,
     asked_smem,
-    zeros,
     chosen,
     profile,
     slope,
@@ -199,6 +204,17 @@
     transmit,
     sums,
     adjoint,
+    wanted,
+    upper,
+    lower,
+    row_of,
+    terms,
+    sharing,
+    field_in,
+    kappa_in,
+    field,
+    east,
+    south,
     block_send,
     block_recv,
     edge_send,
@@ -211,30 +227,30 @@
     barrier = greet_all(me, dev_count, lon_count)
 
     height, breadth, levels = kappa_ref.shape
-    edges = Edges(lat_count, lon_count, kappa_ref, kappa_wide_ref, edge_send, edge_recv)
-    own = pltpu.make_async_copy(
-        kappa_ref, kappa_wide_ref.at[pl.ds(HALO, height), pl.ds(HALO, breadth)], local_sems.at[0]
-    )
-    own.start()
-    zeros[...] = jnp.zeros(zeros.shape, F32)
-
-    def blank(a):
-        rows = pl.ds(0, HALO) if a < 0 else pl.ds(HALO + height, HALO)
-        return pltpu.make_async_copy(zeros, kappa_wide_ref.at[rows], local_sems.at[1])
-
-    for a in (-1, 1):
-
-        @pl.when(jnp.logical_not(edges.there(a)))
-        def _(a=a):
-            blank(a).start()
-            blank(a).wait()
+    tall = height + 2 * HALO
+    count = (breadth + 2 * HALO) // SUB
+    centre = (pl.ds(HALO, height), pl.ds(HALO, breadth))
+    kappa_edges = Edges(
+        lat_count, lon_count, kappa_ref, kappa_in, edge_send.at[0], edge_recv.at[0]
+    )
+    kappa_own = pltpu.make_async_copy(kappa_ref, kappa_in.at[centre], local_sems.at[0])
+    kappa_own.start()
+    is_first = kappa_edges.lat == 0
+    is_last = kappa_edges.lat == lat_count - 1
+    for outside, rows in ((is_first, pl.ds(0, HALO)), (is_last, pl.ds(HALO + height, HALO))):
+
+        @pl.when(outside)
+        def _(rows=rows):
+            kappa_in[rows] = jnp.zeros((HALO,) + kappa_in.shape[1:], F32)
+            field_in[rows] = jnp.zeros((HALO,) + field_in.shape[1:], F32)
+            field[rows] = jnp.zeros((HALO,) + field.shape[1:], F32)
 
     chunk = 256
 
     @pl.loop(0, background_ref.shape[0] // chunk)
     def _(j):
         at = pl.ds(pl.multiple_of(j * chunk, chunk), chunk)
-        field[at, :] = background_ref[at, :].astype(F32)
+        columns[at, :] = background_ref[at, :].astype(F32)
 
     slots = dev_count * cap
     feet, channels = observed_ref.shape
@@ -258,7 +274,7 @@
     scatter_blocks(
         me, lon_count, request_ref, asked_ref, block_send.at[0], block_recv.at[0]
     )
-    edges.start()
+    kappa_edges.start()
 
     block = 256 if slots % 256 == 0 else slots
 
@@ -291,7 +307,7 @@
             total = None
             for k, offset in enumerate((0, 1, tile_cols, tile_cols + 1)):
                 share = asked_smem[source, 0, (k + 1) * cap + r].astype(F32)
-                term = share * field[pl.ds(at + offset, 1), :]
+                term = share * columns[pl.ds(at + offset, 1), :]
                 total = term if total is None else total + term
             found[source, r : r + 1, :] = total * (1.0 / FIXED)
 
@@ -390,99 +406,34 @@
 
 
     scatter_blocks(me, lon_count, found, pulled_ref, block_send.at[2], block_recv.at[2])
-    own.wait()
-    edges.sent()
-    edges.arrive()
-    all_of(request_ref, block_send.at[0])
-    all_of(found, block_send.at[2])
-    all_of(pulled_ref, block_recv.at[2])
-
-
-def spread_kernel(cap, asked_ref, arrived_ref, raw_ref, other):
-    tile_cols = 64
-    cells, levels = raw_ref.shape
-    chunk = 256
-
-    @pl.loop(0, cells // chunk)
-    def _(j):
-        at = pl.ds(pl.multiple_of(j * chunk, chunk), chunk)
-        raw_ref[at, :] = jnp.zeros((chunk, levels), F32)
-        other[at, :] = jnp.zeros((chunk, levels), F32)
-
-    @pl.loop(0, asked_ref.shape[0])
+
+    @pl.loop(0, dev_count)
     def _(source):
-        for r in range(0, cap, 2):
-            for total, row in ((raw_ref, r), (other, r + 1)):
-                at = asked_ref[source, 0, row]
-                value = arrived_ref[source, row : row + 1, :]
-                sites = [pl.ds(at + o, 1) for o in (0, 1, tile_cols, tile_cols + 1)]
-                fresh = []
-                for k in range(4):
-                    share = asked_ref[source, 0, (k + 1) * cap + row].astype(F32)
-                    fresh.append(total[sites[k], :] + share * value)
-                for k in range(4):
-                    total[sites[k], :] = fresh[k]
-
-    @pl.loop(0, cells // chunk)
-    def _(j):
-        at = pl.ds(pl.multiple_of(j * chunk, chunk), chunk)
-        raw_ref[at, :] = (raw_ref[at, :] + other[at, :]) * (-1.0 / FIXED)
-
-
-def diffuse_kernel(
-    lat_count,
-    lon_count,
-    raw_ref,
-    kappa_ref,
-    out_ref,
-    field_in,
-    kappa_in,
-    field,
-    east,
-    south,
-    local_sems,
-    send_sems,
-    recv_sems,
-):
-    height, breadth, levels = raw_ref.shape
-    tall = height + 2 * HALO
-    count = (breadth + 2 * HALO) // SUB
-    edges = Edges(lat_count, lon_count, raw_ref, field_in, send_sems, recv_sems)
-    is_first = edges.lat == 0
-    is_last = edges.lat == lat_count - 1
-
-    barrier = pltpu.get_barrier_semaphore()
-    for a, b in DIRECTIONS:
-
-        @pl.when(edges.there(a))
-        def _(a=a, b=b):
-            pl.semaphore_signal(
-                barrier, inc=1, device_id=edges.device(a, b), device_id_type=MESH
-            )
-
-    centre = (pl.ds(HALO, height), pl.ds(HALO, breadth))
-    kappa_copy = pltpu.make_async_copy(kappa_ref, kappa_in, local_sems.at[0])
-    kappa_copy.start()
-    own = pltpu.make_async_copy(raw_ref, field_in.at[centre], local_sems.at[1])
-    own.start()
-
-    zero_rows = jnp.zeros((HALO, breadth + 2 * HALO, levels), F32)
-    flat_rows = jnp.zeros((HALO, count, SUB, levels), F32)
-
-    @pl.when(is_first)
-    def _():
-        field_in[pl.ds(0, HALO)] = zero_rows
-        field[pl.ds(0, HALO)] = flat_rows
-
-    @pl.when(is_last)
-    def _():
-        field_in[pl.ds(HALO + height, HALO)] = zero_rows
-        field[pl.ds(HALO + height, HALO)] = flat_rows
-
-    neighbours = 8 - 3 * is_first.astype(I32) - 3 * is_last.astype(I32)
-    pl.semaphore_wait(barrier, neighbours)
-    edges.start()
-    kappa_copy.wait()
+        wanted[pl.ds(source, 1), :] = asked_ref[source]
+
+    asked_t = jnp.swapaxes(wanted[...], 0, 1)
+    column = lax.broadcasted_iota(I32, (breadth, dev_count), 0)
+    shift = breadth.bit_length() - 1
+    for r in range(cap):
+        base = asked_t[r : r + 1, :]
+        base_row = lax.shift_right_logical(base, shift)
+        base_col = base - lax.shift_left(base_row, shift)
+        shares = [
+            asked_t[(k + 1) * cap + r : (k + 1) * cap + r + 1, :].astype(F32) * (1.0 / FIXED)
+            for k in range(4)
+        ]
+        at = slice(r * dev_count, (r + 1) * dev_count)
+        row_of[:, at] = base_row.astype(F32)
+        for target, first, second in ((upper, shares[0], shares[1]), (lower, shares[2], shares[3])):
+            taken = jnp.where(column == base_col, first, 0.0)
+            taken = jnp.where(column == base_col + 1, second, taken)
+            high = taken.astype(BF16)
+            target[0:breadth, at] = high
+            target[breadth : 2 * breadth, at] = (taken - high.astype(F32)).astype(BF16)
+
+    kappa_own.wait()
+    kappa_edges.sent()
+    kappa_edges.arrive()
 
     def strided(ref, r):
         return tuple(ref[r, pl.ds(i, SUB, stride=count), :] for i in range(count))
@@ -502,10 +453,62 @@
         return below
 
     lax.fori_loop(0, tall, conduct, strided(kappa_in, 0))
-    own.wait()
+
+    all_of(request_ref, block_send.at[0])
+    all_of(found, block_send.at[2])
+    all_of(pulled_ref, block_recv.at[2])
+
+    slot_rows = pulled_ref.reshape(slots, levels)
+    for r in range(cap):
+        pulled = slot_rows[pl.ds(r, dev_count, stride=cap), :]
+        high = pulled.astype(BF16)
+        at = slice(r * dev_count, (r + 1) * dev_count)
+        terms[at, 0:levels] = high
+        terms[at, levels : 2 * levels] = (pulled - high.astype(F32)).astype(BF16)
+
+    edges = Edges(
+        lat_count,
+        lon_count,
+        field_in.at[centre],
+        field_in,
+        edge_send.at[1],
+        edge_recv.at[1],
+        (height, breadth),
+    )
+    bands = height // HALO
+
+    @pl.loop(0, bands)
+    def _(turn):
+        band = jnp.where(turn == 0, 0, jnp.where(turn == 1, bands - 1, turn - 1))
+        for g in range(HALO):
+            row = (band * HALO + g).astype(F32)
+            in_upper = (row_of[...] == row).astype(F32).astype(BF16)
+            in_lower = (row_of[...] == row - 1.0).astype(F32).astype(BF16)
+            sharing[g * 2 * breadth : (g + 1) * 2 * breadth, :] = (
+                upper[...] * in_upper + lower[...] * in_lower
+            )
+        product = dot(sharing[...], terms[...], ((1,), (0,)))
+        for g in range(HALO):
+            first = g * 2 * breadth
+            second = first + breadth
+            raw = (
+                product[first:second, 0:levels]
+                + product[first:second, levels : 2 * levels]
+                + product[second : second + breadth, 0:levels]
+            )
+            field_in[HALO + band * HALO + g, pl.ds(HALO, breadth), :] = -raw
+        for n, (a, b) in enumerate(DIRECTIONS):
+            if a == 0:
+                edges.copy(n, band).start()
+
+        @pl.when(turn == 1)
+        def _():
+            edges.start(lambda a: a != 0)
+
     edges.arrive()
-
-    def plain(ref, r):
+    edges.sent()
+
+    def whole_rows(ref, r):
         return tuple(ref[r, i] for i in range(count))
 
     for step in range(1, STEPS + 1):
@@ -514,7 +517,7 @@
         if step == 1:
             load = functools.partial(strided, field_in)
         else:
-            load = functools.partial(plain, field)
+            load = functools.partial(whole_rows, field)
 
         def relax(r, carry, load=load, step=step):
             here, above = carry
@@ -538,9 +541,8 @@
         above = tuple(south[low - 1, i] * (here[i] - before[i]) for i in range(count))
         lax.fori_loop(low, high, relax, (here, above))
 
-    result = pltpu.make_async_copy(field_in.at[centre], out_ref, local_sems.at[0])
+    result = pltpu.make_async_copy(field_in.at[centre], increment_ref, local_sems.at[0])
     result.start()
-    edges.sent()
     result.wait()
 
 
@@ -578,22 +580,19 @@
     )(tile_index.reshape(1, feet), anchor.reshape(1, feet), weights.T)
 
     wide = (height + 2 * HALO, breadth + 2 * HALO, levels)
-    asked, departure, pulled, kappa_wide = pl.pallas_call(
+    turned = (wide[0], wide[1] // SUB, SUB, levels)
+    departure, increment = pl.pallas_call(
         functools.partial(observe_kernel, cap, lat_count, lon_count),
-        out_shape=(
-            shape((dev_count, 1, width), I32),
-            shape((feet, channels), F32),
-            shape((dev_count, cap, levels), F32),
-            shape(wide, F32),
-        ),
+        out_shape=(shape((feet, channels), F32), shape((height, breadth, levels), F32)),
         in_specs=[VMEM_SPEC] * 8 + [ANY_SPEC],
-        out_specs=(VMEM_SPEC, VMEM_SPEC, VMEM_SPEC, ANY_SPEC),
+        out_specs=(VMEM_SPEC, ANY_SPEC),
         scratch_shapes=[
+            pltpu.VMEM((dev_count, 1, width), I32),
+            pltpu.VMEM((dev_count, cap, levels), F32),
             pltpu.VMEM((height * breadth, levels), F32),
             pltpu.VMEM((dev_count, cap, levels), F32),
             pltpu.VMEM((dev_count, cap, levels), F32),
             pltpu.SMEM((dev_count, 1, width), I32),
-            pltpu.VMEM((HALO,) + wide[1:], F32),
             pltpu.VMEM((slots, feet), BF16),
             pltpu.VMEM((feet // LANES, levels, LANES), F32),
             pltpu.VMEM((feet // LANES, levels, LANES), F32),
@@ -605,10 +604,21 @@
             pltpu.VMEM((levels, channels, LANES), F32),
             pltpu.VMEM((2, levels * SUB, LANES), F32),
             pltpu.VMEM((levels, feet), F32),
+            pltpu.VMEM((dev_count, width), I32),
+            pltpu.VMEM((2 * breadth, slots), BF16),
+            pltpu.VMEM((2 * breadth, slots), BF16),
+            pltpu.VMEM((1, slots), F32),
+            pltpu.VMEM((slots, 2 * levels), BF16),
+            pltpu.VMEM((HALO * 2 * breadth, slots), BF16),
+            pltpu.VMEM(wide, F32),
+            pltpu.VMEM(wide, F32),
+            pltpu.VMEM(turned, F32),
+            pltpu.VMEM(turned, F32),
+            pltpu.VMEM(turned, F32),
             dma((3,)),
             dma((3,)),
-            dma((8,)),
-            dma((8,)),
+            dma((2, 8)),
+            dma((2, 8)),
             dma((2,)),
         ],
         compiler_params=params(collective_id=0, has_side_effects=True),
@@ -625,35 +635,6 @@
         diffusivity,
     )
 
-    raw = pl.pallas_call(
-        functools.partial(spread_kernel, cap),
-        out_shape=shape((height * breadth, levels), F32),
-        in_specs=[SMEM_SPEC, VMEM_SPEC],
-        out_specs=VMEM_SPEC,
-        scratch_shapes=[pltpu.VMEM((height * breadth, levels), F32)],
-        compiler_params=params(),
-        name="spread",
-    )(asked, pulled)
-
-    turned = (height + 2 * HALO, (breadth + 2 * HALO) // SUB, SUB, levels)
-    increment = pl.pallas_call(
-        functools.partial(diffuse_kernel, lat_count, lon_count),
-        out_shape=shape((height, breadth, levels), F32),
-        in_specs=[ANY_SPEC, ANY_SPEC],
-        out_specs=ANY_SPEC,
-        scratch_shapes=[
-            pltpu.VMEM(wide, F32),
-            pltpu.VMEM(wide, F32),
-            pltpu.VMEM(turned, F32),
-            pltpu.VMEM(turned, F32),
-            pltpu.VMEM(turned, F32),
-            dma((2,)),
-            dma((8,)),
-            dma((8,)),
-        ],
-        compiler_params=params(collective_id=1, has_side_effects=True),
-        name="diffuse",
-    )(raw.reshape(height, breadth, levels), kappa_wide)
     return (departure, increment)
 
 

time: 112 us -> 100 us (0.89)
  Pallas kernels: 108 us -> 94.7 us
    pallas_call x2 -> x0, Pallas kernels: 34.6 us -> none  [the longest x1 25.9 us: local(): pl.pallas_call(functools.partial(diffuse_kernel, lat_count, lon_count), o...]
    pallas_call x1, Pallas kernels: 71 us -> 92.7 us  [local(): pl.pallas_call(functools.partial(observe_kernel, cap, lat_count, lon_coun...]
    unnamed x4 -> x2, local copies, waits for them, and re-layouts: 3.87 us -> 4.83 us
where the time goes in v3:
time: 100 us
  Pallas kernels  94.7 us (95%)
  local copies, waits for them, and re-layouts  4.83 us (5%)
    pallas_call x1, Pallas kernels, local(): pl.pallas_call(functools.partial(observe_kernel, cap, lat_count, lon_coun...  92.7 us
    unnamed x2, local copies, waits for them, and re-layouts  4.83 us

profile of v3, /device:TPU:1, one launch (start us, length us, event | category | flops | bytes accessed | tf_op | source)
XLA Modules:
  0.0 100.1 jit_solution(3946383846686976526)
XLA Ops:
  0.6 2.0 %request.1 = (s32[1,512]{1,0:T(1,128)}, s32[128,1,128]{2,1,0:T(1,128)}) custom-call(s32[1,512]{1,0:T(1,128)} %bitcast.8, s32[1,512]{1,0:T(1,128)} %bitcast.9, f32[4,512]{1,0:T(4,128)} %bitcast.7), custom_call_target="tpu_custom_call" | custom-call | tf_op jit(solution)/shard_map/request/pallas_call | solution.py:573
  2.6 92.7 %observe.1 = (f32[512,128]{1,0:T(8,128)}, f32[64,64,128]{2,1,0:T(8,128)}) custom-call(s32[1,512]{1,0:T(1,128)} %get-tuple-element.4.slot_ref, s32[128,1,128]{2,1,0:T(1,128)} %get-tuple-element.5.request_ref, bf16[4096,128]{1,0:T(8,128)(2,1)} %bitcast.6, f32[512,128]{1,0:T(8,128)} %observed_ref.1, s32[512,128]{1,0:T(8,128)} %accept_ref.1, ...), custom_call_target="tpu_custom_call" | custom-call | tf_op jit(solution)/shard_map/observe/pallas_call | solution.py:584
  95.3 1.7 %copy.14 = f32[512,128]{1,0:T(8,128)} copy(f32[512,128]{1,0:T(8,128)} %get-tuple-element.8) | data formatting | bytes 524288
  97.0 3.2 %copy.15 = f32[64,64,128]{2,1,0:T(8,128)} copy(f32[64,64,128]{2,1,0:T(8,128)} %get-tuple-element.9) | data formatting | bytes 4194304

commit v4 on v3

--- a/solution.py
+++ b/solution.py
@@ -224,7 +224,6 @@
     dev_count = request_ref.shape[0]
     tile_cols = 64
     me = my_index(lon_count)
-    barrier = greet_all(me, dev_count, lon_count)
 
     height, breadth, levels = kappa_ref.shape
     tall = height + 2 * HALO
@@ -245,17 +244,17 @@
             field_in[rows] = jnp.zeros((HALO,) + field_in.shape[1:], F32)
             field[rows] = jnp.zeros((HALO,) + field.shape[1:], F32)
 
+    slots = dev_count * cap
+    feet, channels = observed_ref.shape
+    groups = feet // LANES
+    parts = channels // SUB
+    barrier = greet_all(me, dev_count, lon_count)
     chunk = 256
 
     @pl.loop(0, background_ref.shape[0] // chunk)
     def _(j):
         at = pl.ds(pl.multiple_of(j * chunk, chunk), chunk)
         columns[at, :] = background_ref[at, :].astype(F32)
-
-    slots = dev_count * cap
-    feet, channels = observed_ref.shape
-    groups = feet // LANES
-    parts = channels // SUB
 
     wide = lambda row: jnp.swapaxes(jnp.broadcast_to(row, (LANES, channels)), 0, 1)
     sens = wide(sensitivity_ref[...])
@@ -346,7 +345,7 @@
             return tuple(out)
 
         zero = jnp.zeros((SUB, LANES), F32)
-        done = lax.fori_loop(0, levels, descend, ((zero, zero),) * parts, unroll=4)
+        done = lax.fori_loop(0, levels, descend, ((zero, zero),) * parts, unroll=8)
         top = profile[g, 0:1, :]
         observed_t = jnp.swapaxes(observed_ref[at, :], 0, 1)
         departed = []
@@ -382,7 +381,7 @@
             sums[1, at_l, :] = layer_sum
             return tuple(out)
 
-        lax.fori_loop(0, levels, ascend, (zero,) * parts, unroll=4)
+        lax.fori_loop(0, levels, ascend, (zero,) * parts, unroll=8)
         total = None
         for matrix, index in ((fall, 0), (same, 1)):
             for piece in pieces(sums[index]):
@@ -512,16 +511,16 @@
         return tuple(ref[r, i] for i in range(count))
 
     for step in range(1, STEPS + 1):
-        low = jnp.where(is_first, HALO, step)
+        low = jnp.where(is_first, HALO, jnp.where(is_last, step - step % 2, step))
         high = jnp.where(is_last, HALO + height, tall - step)
         if step == 1:
             load = functools.partial(strided, field_in)
         else:
             load = functools.partial(whole_rows, field)
 
-        def relax(r, carry, load=load, step=step):
+        def relax_row(r, carry, load=load, step=step):
             here, above = carry
-            below = load(r + 1)
+            below = load(jnp.minimum(r + 1, tall - 1))
             down = [south[r, i] * (below[i] - here[i]) for i in range(count)]
             right = []
             for i in range(count):
@@ -536,10 +535,14 @@
                     field[r, i] = new
             return below, tuple(down)
 
-        before = load(low - 1)
+        def relax(turn, carry, relax_row=relax_row, low=low):
+            r = low + 2 * turn
+            return relax_row(r + 1, relax_row(r, carry))
+
+        before = load(jnp.maximum(low - 1, 0))
         here = load(low)
-        above = tuple(south[low - 1, i] * (here[i] - before[i]) for i in range(count))
-        lax.fori_loop(low, high, relax, (here, above))
+        above = tuple(south[jnp.maximum(low - 1, 0), i] * (here[i] - before[i]) for i in range(count))
+        lax.fori_loop(0, (high - low + 1) // 2, relax, (here, above))
 
     result = pltpu.make_async_copy(field_in.at[centre], increment_ref, local_sems.at[0])
     result.start()
@@ -583,9 +586,9 @@
     turned = (wide[0], wide[1] // SUB, SUB, levels)
     departure, increment = pl.pallas_call(
         functools.partial(observe_kernel, cap, lat_count, lon_count),
-        out_shape=(shape((feet, channels), F32), shape((height, breadth, levels), F32)),
+        out_shape=(pltpu.VMEM((feet, channels), F32), pltpu.VMEM((height, breadth, levels), F32)),
         in_specs=[VMEM_SPEC] * 8 + [ANY_SPEC],
-        out_specs=(VMEM_SPEC, ANY_SPEC),
+        out_specs=(VMEM_SPEC, VMEM_SPEC),
         scratch_shapes=[
             pltpu.VMEM((dev_count, 1, width), I32),
             pltpu.VMEM((dev_count, cap, levels), F32),

time: 100 us -> 93.2 us (0.932)
  Pallas kernels: 94.7 us -> 90.3 us
  local copies, waits for them, and re-layouts: 4.83 us -> 2.02 us
    pallas_call x1, Pallas kernels: 92.7 us -> 88.4 us  [local(): pl.pallas_call(functools.partial(observe_kernel, cap, lat_count, lon_coun...]
    unnamed x2, local copies, waits for them, and re-layouts: 4.83 us -> 2.02 us
where the time goes in v4:
time: 93.2 us; the launch traced here: 93 us
  Pallas kernels  90.3 us (97%)
  local copies, waits for them, and re-layouts  2.02 us (2%)
    pallas_call x1, Pallas kernels, local(): pl.pallas_call(functools.partial(observe_kernel, cap, lat_count, lon_coun...  88.4 us
    unnamed x2, local copies, waits for them, and re-layouts  2.02 us
    pallas_call x1, Pallas kernels, local(): pl.pallas_call(functools.partial(request_kernel, cap), out_shape=(shape((...  1.96 us

profile of v4, /device:TPU:1, one launch (start us, length us, event | category | flops | bytes accessed | tf_op | source)
XLA Modules:
  0.0 93.0 jit_solution(5637779453962386044)
XLA Ops:
  0.6 2.0 %request.1 = (s32[1,512]{1,0:T(1,128)}, s32[128,1,128]{2,1,0:T(1,128)}) custom-call(s32[1,512]{1,0:T(1,128)} %bitcast.8, s32[1,512]{1,0:T(1,128)} %bitcast.9, f32[4,512]{1,0:T(4,128)} %bitcast.7), custom_call_target="tpu_custom_call" | custom-call | tf_op jit(solution)/shard_map/request/pallas_call | solution.py:576
  2.6 88.4 %observe.1 = (f32[512,128]{1,0:T(8,128)S(1)}, f32[64,64,128]{2,1,0:T(8,128)S(1)}) custom-call(s32[1,512]{1,0:T(1,128)} %get-tuple-element.4.slot_ref, s32[128,1,128]{2,1,0:T(1,128)} %get-tuple-element.5.request_ref, bf16[4096,128]{1,0:T(8,128)(2,1)} %bitcast.6, f32[512,128]{1,0:T(8,128)} %observed_ref.1, s32[512,128]{1,0:T(8,128)} %accept_ref.1, ...), custom_call_target="tpu_custom_call" | custom-call | tf_op jit(solution)/shard_map/observe/pallas_call | solution.py:587
  91.0 0.7 copy.14
  91.7 1.3 %copy.15 = f32[64,64,128]{2,1,0:T(8,128)} copy(f32[64,64,128]{2,1,0:T(8,128)S(1)} %get-tuple-element.7) | data formatting | bytes 4194304

commit v5 on v4

--- a/solution.py
+++ b/solution.py
@@ -317,9 +317,9 @@
     all_of(found, block_send.at[1])
 
     arrived_t = jnp.swapaxes(arrived[...].reshape(slots, levels), 0, 1)
-    high, middle, low = pieces(arrived_t)
+    high, middle, _ = pieces(arrived_t)
     plain = ((1,), (0,))
-    mine = dot(high, chosen[...], plain) + dot(middle, chosen[...], plain) + dot(low, chosen[...], plain)
+    mine = dot(high, chosen[...], plain) + dot(middle, chosen[...], plain)
     below = jnp.concatenate([mine[1:, :], mine[levels - 1 :, :]], axis=0)
     for g in range(groups):
         at = slice(g * LANES, (g + 1) * LANES)
@@ -345,7 +345,7 @@
             return tuple(out)
 
         zero = jnp.zeros((SUB, LANES), F32)
-        done = lax.fori_loop(0, levels, descend, ((zero, zero),) * parts, unroll=8)
+        done = lax.fori_loop(0, levels, descend, ((zero, zero),) * parts, unroll=16)
         top = profile[g, 0:1, :]
         observed_t = jnp.swapaxes(observed_ref[at, :], 0, 1)
         departed = []
@@ -381,7 +381,7 @@
             sums[1, at_l, :] = layer_sum
             return tuple(out)
 
-        lax.fori_loop(0, levels, ascend, (zero,) * parts, unroll=8)
+        lax.fori_loop(0, levels, ascend, (zero,) * parts, unroll=16)
         total = None
         for matrix, index in ((fall, 0), (same, 1)):
             for piece in pieces(sums[index]):
@@ -390,7 +390,7 @@
         first = lax.broadcasted_iota(I32, (levels, LANES), 0) == 0
         adjoint[:, at] = total + jnp.where(first, whole, 0.0)
 
-    parts_adjoint = pieces(adjoint[...])
+    parts_adjoint = pieces(adjoint[...])[:2]
 
     @pl.loop(0, slots // block)
     def _(j):

time: 93.2 us -> 92.2 us (0.989)
  no operation moved by 1% of the time
where the time goes in v5:
time: 92.2 us; the launch traced here: 92.1 us
  Pallas kernels  89.4 us (97%)
  local copies, waits for them, and re-layouts  2.02 us (2%)
    pallas_call x1, Pallas kernels, local(): pl.pallas_call(functools.partial(observe_kernel, cap, lat_count, lon_coun...  87.4 us
    unnamed x2, local copies, waits for them, and re-layouts  2.02 us
    pallas_call x1, Pallas kernels, local(): pl.pallas_call(functools.partial(request_kernel, cap), out_shape=(shape((...  1.96 us

profile of v5, /device:TPU:1, one launch (start us, length us, event | category | flops | bytes accessed | tf_op | source)
XLA Modules:
  0.0 92.1 jit_solution(14897189357878194454)
XLA Ops:
  0.6 2.0 %request.1 = (s32[1,512]{1,0:T(1,128)}, s32[128,1,128]{2,1,0:T(1,128)}) custom-call(s32[1,512]{1,0:T(1,128)} %bitcast.8, s32[1,512]{1,0:T(1,128)} %bitcast.9, f32[4,512]{1,0:T(4,128)} %bitcast.7), custom_call_target="tpu_custom_call" | custom-call | tf_op jit(solution)/shard_map/request/pallas_call | solution.py:576
  2.6 87.4 %observe.1 = (f32[512,128]{1,0:T(8,128)S(1)}, f32[64,64,128]{2,1,0:T(8,128)S(1)}) custom-call(s32[1,512]{1,0:T(1,128)} %get-tuple-element.4.slot_ref, s32[128,1,128]{2,1,0:T(1,128)} %get-tuple-element.5.request_ref, bf16[4096,128]{1,0:T(8,128)(2,1)} %bitcast.6, f32[512,128]{1,0:T(8,128)} %observed_ref.1, s32[512,128]{1,0:T(8,128)} %accept_ref.1, ...), custom_call_target="tpu_custom_call" | custom-call | tf_op jit(solution)/shard_map/observe/pallas_call | solution.py:587
  90.0 0.7 copy.14
  90.7 1.3 %copy.15 = f32[64,64,128]{2,1,0:T(8,128)} copy(f32[64,64,128]{2,1,0:T(8,128)S(1)} %get-tuple-element.7) | data formatting | bytes 4194304
